TPU v7x, 256 devices: a whole 4x4x8 slice. The times are simulated.
256 devices in a mesh: seg: 8 (over y_hi, x), blk: 32 (over z, y_lo, core).
Axes of the slice: x: 4, y: 4 (y_hi: 2, y_lo: 2; y = y_hi * 2 + y_lo), z: 8, core: 2. Of those that a mesh axis runs over, the one named last changes fastest.
Arguments:
- state: float32 [256, 4, 16, 2304], P(('seg', 'blk')), may hold values from -6 to 6
- metric: float32 [256, 9, 16, 2304], P(('seg', 'blk')), may hold values from -0.4 to 3, as said below
- block_map: int32 [256], replicated, may hold values from 0 to 255, as said below
- links: int32 [256, 6, 4], replicated, may hold values from -1 to 255, as said below
Outputs:
- advanced: float32 [256, 4, 16, 2304], P(('seg', 'blk'))
Inputs may be any that keep to these rules, and one draw needn't show every extreme that they name: A permutation of the block numbers; device slot d = s * 32 + p (segment s, position p along its chain) holds block block_map[d]. `links`: entries are (partner block or -1, partner face, r_i, r_x). Face 0 of the block at position p > 0 joins face 1 of the block at position p - 1 of the same segment, face 1 at p < 31 joins face 0 at p + 1, both with zero flags; faces 0 at p = 0 and 1 at p = 31 have partner -1. A block has at most one of faces 2 to 5 with a partner, and some blocks have one; that partner lies at the same position p in another segment, names this block and face back with the same flags. Unused fields of a face with partner -1 are 0. `metric`: entries 0, 4 and 8 of the second dimension are positive.
All inputs are finite; a program needn't handle non-finite values.
Results may differ from a plain program's by a relative error of at most 0.0003.
Values sent between devices are 32-bit elements; how exact they have to be, the bound alone decides.
No kernel may reach another device: no remote copies, remote signals or barrier semaphores. Data moves between devices by JAX's collectives and lax.ppermute only.
A program may use at most 64 MiB of HBM per device.

v0:
```python
import functools
import jax
import jax.numpy as jnp
from jax import lax
from jax.experimental import pallas as pl
from jax.experimental.pallas import tpu as pltpu
from jax.sharding import PartitionSpec as P

LEN, CROSS, CELLS, TILES = 16, 48, 2304, 18
GROUP = 6
GEOMETRY, BELOW, ABOVE, ROWS = 64, 208, 216, 224
USED, SPARE = 96, 32
FACE, ALONG, ACROSS, POSITION, HAS_LOW, HAS_HIGH, OWN, MATE = 0, 1, 2, 3, 4, 5, 6, 9
PARTS = ((0, BELOW), (BELOW, ABOVE), (ABOVE, ROWS))
SEGS, CHAIN = 8, 32
time_step = 0.05
viscosity = 0.2
compress = 1.0
SIGN = (-1.0, -1.0, -1.0, 1.0)
VMEM = pl.BlockSpec(memory_space=pltpu.VMEM)
SMEM = pl.BlockSpec(memory_space=pltpu.SMEM)


def lanes_of(rows=8):
    return lax.broadcasted_iota(jnp.int32, (rows, 128), 1)


def gather_lanes(values, index):
    parts = [
        jnp.take_along_axis(values[r : r + 8], index, axis=1, mode="promise_in_bounds")
        for r in range(0, values.shape[0], 8)
    ]
    return parts[0] if len(parts) == 1 else jnp.concatenate(parts, axis=0)


def reversed_rows(values):
    index = 7 - lax.broadcasted_iota(jnp.int32, (8, 128), 0)
    flip = lambda part: jnp.take_along_axis(part, index, axis=0, mode="promise_in_bounds")
    return jnp.concatenate([flip(values[8:16]), flip(values[0:8])], axis=0)


def joined_face(device, block_map, links):
    block = block_map[device]
    face, partner, along, across = jnp.int32(0), jnp.int32(-1), jnp.int32(0), jnp.int32(0)
    for side in range(2, 6):
        other = links[side, 0, block]
        here = other >= 0
        face = jnp.where(here, side, face)
        partner = jnp.where(here, other, partner)
        along = jnp.where(here, links[side, 2, block], along)
        across = jnp.where(here, links[side, 3, block], across)
    position = lax.rem(device, CHAIN)
    segment = jnp.int32(0)
    for s in range(SEGS):
        segment = jnp.where(block_map[s * CHAIN + position] == partner, s, segment)
    return face, segment, along, across


def face_source(face, across, first_layer):
    lane = lanes_of()
    layer = jnp.where(lane >= CROSS, 1, 0)
    place = lane - layer * CROSS
    place = jnp.where(across == 1, CROSS - 1 - place, place)
    depth = first_layer + layer
    depth = jnp.where((face == 3) | (face == 5), CROSS - 1 - depth, depth)
    return jnp.where(face <= 3, depth * CROSS + place, place * CROSS + depth)


def gather_face(load, source):
    index, owner = source & 127, source >> 7
    found = None
    for t in range(TILES):
        picked = gather_lanes(load(t), index)
        if found is None:
            found = picked
        else:
            inside = owner == t
            if picked.shape[0] == LEN:
                inside = jnp.concatenate([inside, inside], axis=0)
            found = jnp.where(inside, picked, found)
    return found


def write_chain(field, even_ref, odd_ref, position):
    even = lax.rem(position, 2) == 0
    for c in range(4):
        low, high = field[c, 0:2, :], field[c, LEN - 2 : LEN, :]
        even_ref[2 * c : 2 * c + 2, 0:CELLS] = jnp.where(even, high, low)
        odd_ref[2 * c : 2 * c + 2, 0:CELLS] = jnp.where(even, low, high)


def first_kernel(
    q_hbm, metric_hbm, map_hbm, links_hbm, q, metric, joint_ref, even_ref, odd_ref, meta, block_map, links, sem
):
    copies = [
        pltpu.make_async_copy(source, target, sem.at[n])
        for n, (source, target) in enumerate(
            ((links_hbm, links), (map_hbm, block_map), (q_hbm, q), (metric_hbm, metric))
        )
    ]
    for copy in copies:
        copy.start()
    segment, position = lax.axis_index("seg"), lax.axis_index("blk")
    copies[0].wait()
    copies[1].wait()
    here = segment * CHAIN + position
    other = (segment ^ 4) * CHAIN + position
    before, after = jnp.where(position > 0, -1, 0), jnp.where(position < CHAIN - 1, 1, 0)
    face, partner, along, across = joined_face(here, block_map, links)
    low_face, low_partner, _, low_across = joined_face(here + before, block_map, links)
    high_face, high_partner, _, high_across = joined_face(here + after, block_map, links)
    own = (partner, low_partner, high_partner)
    mates = [joined_face(other + shift, block_map, links)[1] for shift in (0, before, after)]
    meta[FACE] = face
    meta[ALONG] = along
    meta[ACROSS] = across
    meta[POSITION] = position
    block = block_map[here]
    meta[HAS_LOW] = jnp.where(links[0, 0, block] >= 0, 1, 0)
    meta[HAS_HIGH] = jnp.where(links[1, 0, block] >= 0, 1, 0)
    for n in range(3):
        meta[OWN + n] = jnp.where(own[n] // 4 == segment // 4, (own[n] ^ segment) & 3, 0)
        meta[MATE + n] = (mates[n] ^ segment) & 3
    copies[2].wait()
    write_chain(q, even_ref, odd_ref, position)

    where = lambda t: slice(128 * t, 128 * t + 128)
    lane = lanes_of(LEN)
    near, deep = face_source(face, across, 0), face_source(face, across, 2)
    below, above = face_source(low_face, low_across, 0), face_source(high_face, high_across, 0)
    deeper = [gather_face(lambda t: q[c, :, where(t)], deep) for c in range(4)]

    def put(n, values):
        if n < 12:
            third = pltpu.roll(deeper[n // 3], USED - SPARE * (n % 3), 1)
            values = jnp.where(lane < USED, values, third)
        joint_ref[LEN * n : LEN * n + LEN, :] = jnp.where(along == 1, reversed_rows(values), values)

    for c in range(4):
        put(c, gather_face(lambda t: q[c, :, where(t)], near))
        low_rows = gather_face(lambda t: q[c, 0:8, where(t)], below)
        joint_ref[BELOW + 2 * c : BELOW + 2 * c + 2, :] = low_rows[0:2]
        high_rows = gather_face(lambda t: q[c, 8:16, where(t)], above)
        joint_ref[ABOVE + 2 * c : ABOVE + 2 * c + 2, :] = high_rows[6:8]
    copies[3].wait()
    normal = jnp.where(face <= 3, 1, 2)
    inward = jnp.where((face == 3) | (face == 5), -1.0, 1.0)
    forward = jnp.where(along == 1, -1.0, 1.0)
    sideways = jnp.where(across == 1, -1.0, 1.0)
    for a, (row, sign) in enumerate(((0, forward), (3 * normal, inward), (3 * (3 - normal), sideways))):
        for b in range(3):
            found = gather_face(lambda t: metric[row + b, :, where(t)], near)
            put(4 + 3 * a + b, sign * found)


def copy_part(choice, refs, rows, out):
    for n, ref in enumerate(refs):

        @pl.when(choice == n)
        def _(ref=ref):
            out[...] = ref[rows[0] : rows[1], :]


def pick_kernel(own, one, two, three, meta, out):
    for n, rows in enumerate(PARTS):
        copy_part(meta[MATE + n], (own, one, two, three), rows, out.at[rows[0] : rows[1], :])


def shifted_lanes(before, here, after, shift):
    lane = lanes_of(LEN)
    if shift > 0:
        return jnp.where(
            lane < 128 - shift, pltpu.roll(here, 128 - shift, 1), pltpu.roll(after, 128 - shift, 1)
        )
    return jnp.where(lane >= -shift, pltpu.roll(here, -shift, 1), pltpu.roll(before, -shift, 1))


def shifted_rows(padded, shift):
    return pltpu.roll(padded, (-shift) % 32, 0)[8:24]


def differences(m2, m1, here, p1, p2):
    return 8.0 * (p1 - m1) - (p2 - m2)


def bends(m2, m1, here, p1, p2):
    return 16.0 * (p1 + m1) - (p2 + m2) - 30.0 * here


def advance(stencils, geometry):
    here = [stencils[c][0][2] for c in range(4)]
    moves = [-(time_step / 12.0) * geometry[n] for n in range(9)]
    result = list(here)
    fall = None
    for a in range(3):
        g = geometry[3 * a : 3 * a + 3]
        n = moves[3 * a : 3 * a + 3]
        speed = n[0] * here[0] + n[1] * here[1] + n[2] * here[2]
        spread = (viscosity * time_step / 12.0) * (g[0] * g[0] + g[1] * g[1] + g[2] * g[2])
        drop = differences(*stencils[3][a])
        for b in range(3):
            slope = differences(*stencils[b][a])
            result[b] = result[b] + speed * slope + n[b] * drop + spread * bends(*stencils[b][a])
            term = n[b] * slope
            fall = term if fall is None else fall + term
    result[3] = result[3] + compress * fall
    return result


def chain_ghosts(q, even_in, odd_in, meta, low_ref, high_ref):
    even = lax.rem(meta[POSITION], 2) == 0
    for c in range(4):
        rows = slice(2 * c, 2 * c + 2)
        from_even, from_odd = even_in[rows, :], odd_in[rows, :]
        low_ref[c, 6:8, :] = jnp.where(even, from_odd, from_even)
        high_ref[c, 0:2, :] = jnp.where(even, from_even, from_odd)

    @pl.when(meta[HAS_LOW] == 0)
    def _():
        for c in range(4):
            low_ref[c, 7:8, :] = -SIGN[c] * q[c, 0:1, :]
            low_ref[c, 6:7, :] = -SIGN[c] * q[c, 1:2, :]

    @pl.when(meta[HAS_HIGH] == 0)
    def _():
        for c in range(4):
            high_ref[c, 0:1, :] = -SIGN[c] * q[c, LEN - 1 : LEN, :]
            high_ref[c, 1:2, :] = -SIGN[c] * q[c, LEN - 2 : LEN - 1, :]


def bulk_kernel(last, q, metric, *rest):
    if last:
        first, meta, out = rest
    else:
        even_in, odd_in, meta, out, low_ref, high_ref = rest
        chain_ghosts(q, even_in, odd_in, meta, low_ref, high_ref)
    lane = lanes_of(LEN)
    row = lax.broadcasted_iota(jnp.int32, (8, 128), 0)
    face, ends = meta[FACE], (meta[HAS_LOW] == 0, meta[HAS_HIGH] == 0)
    load = lambda c, t: q[c, :, 128 * t : 128 * t + 128]
    before_first, after_last = [], []
    for c in range(4):
        head = jnp.where(face == 2, 0.0, SIGN[c]) * load(c, 0)
        before_first.append(jnp.where(lane >= 80, pltpu.roll(head, 80, 1), pltpu.roll(head, 112, 1)))
        tail = jnp.where(face == 3, 0.0, SIGN[c]) * load(c, TILES - 1)
        after_last.append(jnp.where(lane < CROSS, pltpu.roll(tail, 48, 1), pltpu.roll(tail, 16, 1)))

    def tile(c, t):
        return before_first[c] if t < 0 else after_last[c] if t >= TILES else load(c, t)

    low_scale = jnp.where(face == 4, 0.0, 1.0)
    high_scale = jnp.where(face == 5, 0.0, 1.0)
    open_low = jnp.where(ends[0], 1.0, 0.0)
    open_high = jnp.where(ends[1], 1.0, 0.0)
    for t in range(TILES):
        flat = 128 * t + lane
        k = flat - (flat // CROSS) * CROSS
        scale = jnp.where(k < 2, low_scale, high_scale)
        where = slice(128 * t, 128 * t + 128)
        stencils = []
        for c in range(4):
            before, here, after = tile(c, t - 1), tile(c, t), tile(c, t + 1)
            if last:
                top, bottom = here[0:8], here[8:16]
                low = -SIGN[c] * open_low * jnp.where(row == 7, pltpu.roll(top, 7, 0), pltpu.roll(top, 5, 0))
                high = -SIGN[c] * open_high * jnp.where(row == 0, pltpu.roll(bottom, 1, 0), pltpu.roll(bottom, 3, 0))
            else:
                low, high = low_ref[c, :, where], high_ref[c, :, where]
            rows = jnp.concatenate([low, here, high], axis=0)
            along_i = [shifted_rows(rows, s) for s in (-2, -1)] + [here] + [shifted_rows(rows, s) for s in (1, 2)]
            along_j = [shifted_lanes(before, here, after, CROSS * s) if s else here for s in range(-2, 3)]
            raw = [shifted_lanes(before, here, after, s) if s else here for s in range(-2, 3)]
            factor = SIGN[c] * scale
            nearest = factor * here
            second = factor * jnp.where((k == 0) | (k == 46), raw[3], raw[1])
            along_k = [
                jnp.where(k < 2, second, raw[0]),
                jnp.where(k == 0, nearest, raw[1]),
                here,
                jnp.where(k == 47, nearest, raw[3]),
                jnp.where(k >= 46, second, raw[4]),
            ]
            stencils.append((along_i, along_j, along_k))
        values = advance(stencils, [metric[n, :, where] for n in range(9)])
        for c in range(4):
            kept = 0.5 * first[c, :, where] + 0.5 * values[c] if last else values[c]
            out[c, :, where] = kept


def edge_terms(here, geometry, slopes, curves, scale):
    moves = [-(scale * time_step / 12.0) * g for g in geometry]
    speed = moves[0] * here[0] + moves[1] * here[1] + moves[2] * here[2]
    squares = geometry[0] * geometry[0] + geometry[1] * geometry[1] + geometry[2] * geometry[2]
    spread = (scale * viscosity * time_step / 12.0) * squares
    added = [speed * slopes[b] + moves[b] * slopes[3] + spread * curves[b] for b in range(3)]
    added.append(compress * (moves[0] * slopes[0] + moves[1] * slopes[1] + moves[2] * slopes[2]))
    return added


def partner_face(sent, main, low_ref, high_ref, from_low, from_high, meta, ghost_ref):
    lane = lanes_of(LEN)
    place = jnp.where(lane >= CROSS, lane - CROSS, lane)
    along, across = meta[ALONG] == 1, meta[ACROSS] == 1
    missing_low = jnp.where(along, meta[HAS_HIGH], meta[HAS_LOW]) == 0
    missing_high = jnp.where(along, meta[HAS_LOW], meta[HAS_HIGH]) == 0
    mirrored = jnp.where(lane < CROSS, CROSS - 1 - lane, jnp.where(lane < 2 * CROSS, 3 * CROSS - 1 - lane, lane))[:8]
    stencils = []
    for c in range(4):
        mine = sent[LEN * c : LEN * c + LEN, :]
        mine = jnp.where(across, gather_lanes(mine, mirrored), mine)
        mine = jnp.where(along, reversed_rows(mine), mine)
        here = main[LEN * c : LEN * c + LEN, :]
        thirds = [
            pltpu.roll(main[LEN * n : LEN * n + LEN, :], (SPARE * (n % 3) - USED) % 128, 1) for n in range(3 * c, 3 * c + 3)
        ]
        deep = jnp.where(lane < SPARE, thirds[0], jnp.where(lane < 2 * SPARE, thirds[1], thirds[2]))
        below, above = from_low[2 * c : 2 * c + 2, :], from_high[2 * c : 2 * c + 2, :]
        low_ref[6:7, :] = jnp.where(missing_low, -SIGN[c] * here[1:2], jnp.where(along, above[1:2], below[0:1]))
        low_ref[7:8, :] = jnp.where(missing_low, -SIGN[c] * here[0:1], jnp.where(along, above[0:1], below[1:2]))
        high_ref[0:1, :] = jnp.where(missing_high, -SIGN[c] * here[15:16], jnp.where(along, below[1:2], above[0:1]))
        high_ref[1:2, :] = jnp.where(missing_high, -SIGN[c] * here[14:15], jnp.where(along, below[0:1], above[1:2]))
        rows = jnp.concatenate([low_ref[...], here, high_ref[...]], axis=0)
        along_i = [shifted_rows(rows, s) for s in (-2, -1)] + [here] + [shifted_rows(rows, s) for s in (1, 2)]
        outer = lane < CROSS
        normal = [
            jnp.where(outer, pltpu.roll(mine, 80, 1), pltpu.roll(mine, 48, 1)),
            jnp.where(outer, mine, pltpu.roll(here, 48, 1)),
            here,
            jnp.where(outer, pltpu.roll(here, 80, 1), pltpu.roll(deep, 48, 1)),
            deep,
        ]
        raw = [pltpu.roll(here, (-s) % 128, 1) if s else here for s in range(-2, 3)]
        wall = SIGN[c] * here
        second = SIGN[c] * jnp.where((place == 0) | (place == 46), raw[3], raw[1])
        sideways = [
            jnp.where(place < 2, second, raw[0]),
            jnp.where(place == 0, wall, raw[1]),
            here,
            jnp.where(place == 47, wall, raw[3]),
            jnp.where(place >= 46, second, raw[4]),
        ]
        stencils.append((along_i, normal, sideways))
    geometry = [main[GEOMETRY + LEN * n : GEOMETRY + LEN * n + LEN, :] for n in range(9)]
    for c, values in enumerate(advance(stencils, geometry)):
        ghost_ref[LEN * c : LEN * c + LEN, :] = values


def chain_terms(q, metric, chain_ref, scale, tiles, base, out):
    row = lax.broadcasted_iota(jnp.int32, (8, 128), 0)
    start = row < 4
    toward = jnp.where(start, -1.0, 1.0)
    for t in tiles:
        where = slice(128 * t, 128 * t + 128)
        ends = lambda ref, n: jnp.where(start, ref[n, 0:8, where], ref[n, 8:16, where])
        slopes, curves = [], []
        for c in range(4):
            second = chain_ref[c, :, where]
            first = jnp.where(row == 0, pltpu.roll(second, 7, 0), jnp.where(row == 7, pltpu.roll(second, 1, 0), 0.0))
            slopes.append(toward * (8.0 * first - second))
            curves.append(16.0 * first - second)
        added = edge_terms([ends(q, c) for c in range(4)], [ends(metric, n) for n in range(3)], slopes, curves, scale)
        for c in range(4):
            out[c, 0:8, where] = base[c, 0:8, where] + jnp.where(start, added[c], 0.0)
            out[c, 8:16, where] = base[c, 8:16, where] + jnp.where(start, 0.0, added[c])


def joint_terms(q, metric, ghost_ref, face, scale, tiles, out):
    lane = lanes_of(LEN)

    def add(t, direction, slopes, curves):
        where = slice(128 * t, 128 * t + 128)
        here = [q[c, :, where] for c in range(4)]
        geometry = [metric[3 * direction + n, :, where] for n in range(3)]
        added = edge_terms(here, geometry, slopes, curves, scale)
        for c in range(4):
            out[c, :, where] = out[c, :, where] + added[c]

    ghost_of = lambda c: ghost_ref[16 * c : 16 * c + 16, :]
    if tiles[0] == 0:

        @pl.when(face == 2)
        def _():
            slopes, curves = [], []
            for c in range(4):
                ghost = ghost_of(c)
                first = jnp.where(lane < CROSS, ghost, 0.0)
                second = jnp.where(lane < CROSS, pltpu.roll(ghost, 80, 1), pltpu.roll(ghost, 48, 1))
                second = jnp.where(lane < 2 * CROSS, second, 0.0)
                slopes.append(second - 8.0 * first)
                curves.append(16.0 * first - second)
            add(0, 1, slopes, curves)

    if tiles[-1] == TILES - 1:

        @pl.when(face == 3)
        def _():
            slopes, curves = [], []
            for c in range(4):
                ghost = ghost_of(c)
                first = jnp.where(lane >= 80, pltpu.roll(ghost, 80, 1), 0.0)
                second = jnp.where(lane >= 32, pltpu.roll(ghost, 32, 1), 0.0)
                slopes.append(8.0 * first - second)
                curves.append(16.0 * first - second)
            add(TILES - 1, 1, slopes, curves)

    @pl.when(face >= 4)
    def _():
        toward = jnp.where(face == 4, -1.0, 1.0)
        for t in tiles:
            flat = 128 * t + lane
            j = flat // CROSS
            k = flat - j * CROSS
            depth = jnp.where(face == 4, k, CROSS - 1 - k)
            far = jnp.where(depth == 0, j + CROSS, j)[:8]
            slopes, curves = [], []
            for c in range(4):
                ghost = ghost_of(c)
                first = jnp.where(depth == 0, gather_lanes(ghost, j[:8]), 0.0)
                second = jnp.where(depth < 2, gather_lanes(ghost, far), 0.0)
                slopes.append(toward * (8.0 * first - second))
                curves.append(16.0 * first - second)
            add(t, 2, slopes, curves)


def joint_kernel(bulk, q, metric, one, two, three, mate, meta, out, even_ref, odd_ref, ghost_ref, below, above):
    received = (mate, one, two, three)
    copy_part(meta[OWN], received, (0, GEOMETRY), ghost_ref)
    copy_part(meta[OWN + 1], received, PARTS[1], below)
    copy_part(meta[OWN + 2], received, PARTS[2], above)
    out[...] = bulk[...]
    joint_terms(q, metric, ghost_ref, meta[FACE], 1.0, range(TILES), out)
    write_chain(out, even_ref, odd_ref, meta[POSITION])
    even = lax.rem(meta[POSITION], 2) == 0
    spare = slice(CELLS, CELLS + 128)
    even_ref[:, spare] = jnp.where(even, above[...], below[...])
    odd_ref[:, spare] = jnp.where(even, below[...], above[...])


def spread_ghosts(even_in, odd_in, meta, chain_ref):
    even = lax.rem(meta[POSITION], 2) == 0
    has_low = jnp.where(meta[HAS_LOW] == 1, 1.0, 0.0)
    has_high = jnp.where(meta[HAS_HIGH] == 1, 1.0, 0.0)
    for c in range(4):
        rows = slice(2 * c, 2 * c + 2)
        from_even, from_odd = even_in[rows, 0:CELLS], odd_in[rows, 0:CELLS]
        chain_ref[c, 2:6, :] = jnp.zeros((4, CELLS), jnp.float32)
        chain_ref[c, 0:2, :] = has_low * jnp.where(even, from_odd, from_even)
        chain_ref[c, 6:8, :] = has_high * jnp.where(even, from_even, from_odd)


def last_kernel(part, sent, q, metric, one, two, three, mate, even_in, odd_in, meta, out_hbm, *scratch):
    chain_ref, ghost_ref, main, first_low, first_high, out, sem = scratch
    even = lax.rem(meta[POSITION], 2) == 0
    copy_part(meta[OWN], (mate, one, two, three), PARTS[0], main)
    spare = slice(CELLS, CELLS + 128)
    from_even, from_odd = even_in[:, spare], odd_in[:, spare]
    from_low, from_high = jnp.where(even, from_odd, from_even), jnp.where(even, from_even, from_odd)
    partner_face(sent, main, first_low, first_high, from_low, from_high, meta, ghost_ref)
    spread_ghosts(even_in, odd_in, meta, chain_ref)
    copies = []
    for n in range(TILES // GROUP):
        tiles = range(GROUP * n, GROUP * n + GROUP)
        chain_terms(q, metric, chain_ref, 0.5, tiles, part, out)
        joint_terms(q, metric, ghost_ref, meta[FACE], 0.5, tiles, out)
        where = slice(128 * GROUP * n, 128 * GROUP * (n + 1))
        copies.append(pltpu.make_async_copy(out.at[:, :, where], out_hbm.at[:, :, where], sem.at[n]))
        copies[-1].start()
    for copy in copies:
        copy.wait()


f32 = functools.partial(jax.ShapeDtypeStruct, dtype=jnp.float32)
PARAMS = pltpu.CompilerParams(vmem_limit_bytes=24 * 1024 * 1024)
FIELD = f32((4, LEN, CELLS))
JOINT = f32((ROWS, 128))
CHAIN_TILES = pltpu.VMEM((4, 8, CELLS), jnp.float32)
GHOST = pltpu.VMEM((GEOMETRY, 128), jnp.float32)
TILE = pltpu.VMEM((8, 128), jnp.float32)


def local(kernel, shapes, operands, scratch=(), flops=1_000_000, **options):
    options.setdefault("out_specs", [VMEM] * len(shapes))
    return pl.pallas_call(
        kernel,
        out_shape=shapes,
        in_specs=[VMEM] * (len(operands) - 1) + [SMEM],
        scratch_shapes=list(scratch),
        compiler_params=PARAMS,
        cost_estimate=pl.CostEstimate(flops=flops, bytes_accessed=flops, transcendentals=0),
        **options,
    )(*operands)


def bulk(last, *operands):
    kernel = functools.partial(bulk_kernel, last)
    return local(kernel, [FIELD], operands, [] if last else [CHAIN_TILES] * 2, flops=12_000_000)[0]


def along_chain(even, odd):
    pairs = [(i, i + 1) for i in range(1, CHAIN - 1, 2)]
    from_odd = lax.ppermute(odd, "blk", pairs + [(b, a) for a, b in pairs])
    return lax.ppermute(even, "blk", [(i, i ^ 1) for i in range(CHAIN)]), from_odd


def on_device(state, metric, block_map, links):
    HBM = pl.BlockSpec(memory_space=pltpu.HBM)
    held = lambda x: pltpu.with_memory_space_constraint(x, pltpu.HBM)
    arrays = (state.reshape(4, LEN, CELLS), metric.reshape(9, LEN, CELLS), block_map, jnp.transpose(links, (1, 2, 0)))
    q, geometry, joint, even, odd, meta = pl.pallas_call(
        first_kernel,
        out_shape=[FIELD, f32((9, LEN, CELLS)), JOINT] + [f32((8, CELLS))] * 2 + [jax.ShapeDtypeStruct((16,), jnp.int32)],
        in_specs=[HBM] * 4,
        out_specs=[VMEM] * 5 + [SMEM],
        scratch_shapes=[
            pltpu.SMEM((SEGS * CHAIN,), jnp.int32),
            pltpu.SMEM((6, 4, SEGS * CHAIN), jnp.int32),
            pltpu.SemaphoreType.DMA((4,)),
        ],
        compiler_params=PARAMS,
    )(*map(held, arrays))
    across = lambda value, s: lax.ppermute(value, "seg", [(i, i ^ s) for i in range(SEGS)])
    from_even, from_odd = along_chain(even, odd)
    two, three = across(joint, 2), across(joint, 3)
    later, from_odd = lax.optimization_barrier((joint, from_odd))
    one = across(later, 1)
    one, two, three, from_even = lax.optimization_barrier((one, two, three, from_even))
    (picked,) = local(pick_kernel, [JOINT], (joint, one, two, three, meta))
    mate = lax.ppermute(picked, "seg", [(i, i ^ 4) for i in range(SEGS)])
    from_even, from_odd, _ = lax.optimization_barrier((from_even, from_odd, picked))
    part = bulk(False, q, geometry, from_even, from_odd, meta)
    q1, even, odd = local(
        joint_kernel,
        [FIELD] + [f32((8, CELLS + 128))] * 2,
        (part, q, geometry, one, two, three, mate, meta),
        [GHOST, TILE, TILE],
    )
    from_even, from_odd = along_chain(even, odd)
    part = bulk(True, q1, geometry, q, meta)
    (advanced,) = local(
        last_kernel,
        [FIELD],
        (part, joint, q1, geometry, one, two, three, mate, from_even, from_odd, meta),
        [CHAIN_TILES, GHOST, pltpu.VMEM((BELOW, 128), jnp.float32), TILE, TILE]
        + [pltpu.VMEM((4, LEN, CELLS), jnp.float32), pltpu.SemaphoreType.DMA((TILES // GROUP,))],
        out_specs=[HBM],
    )
    return advanced.reshape(state.shape)


def solution(mesh):
    in_specs = (P(("seg", "blk"), None, None, None), P(("seg", "blk"), None, None, None), P(), P())
    out_specs = P(("seg", "blk"), None, None, None)
    return jax.shard_map(
        on_device, mesh=mesh, in_specs=in_specs, out_specs=out_specs, check_vma=False
    )
```

profile of v0, /device:TPU:105, one launch (start us, length us, event | category | flops | bytes accessed | tf_op | source)
XLA Modules:
  0.0 34.4 jit_solution(8446491021641474678)
XLA Ops:
  0.0 2.5 %shard_map.46 = (f32[4,16,2304]{2,1,0:T(8,128)S(1)}, f32[9,16,2304]{2,1,0:T(8,128)S(1)}, f32[224,128]{1,0:T(8,128)S(1)}, f32[8,2304]{1,0:T(8,128)S(1)}, f32[8,2304]{1,0:T(8,128)S(1)}, /*index=5*/s32[16]{0:T(128)S(1)}) custom-call(f32[4,16,2304]{2,1,0:T(8,128)} %bitcast.5, f32[9,16,2304]{2,1,0:T(8,128)} %bitcast.4, s32[256]{0:T(256)} %map_hbm.1, ...), custom_call_target="tpu_custom_call" | custom-call | tf_op jit(solution)/shard_map/pallas_call | solution.py:509
  2.5 5.2 %collective-permute-start = (f32[8,2304]{1,0:T(8,128)S(1)}, f32[8,2304]{1,0:T(8,128)S(1)}, u32[]{:S(2)}, u32[]{:S(2)}) collective-permute-start(f32[8,2304]{1,0:T(8,128)S(1)} %get-tuple-element.25), channel_id=1, source_target_pairs={{1,2},{3,4},{5,6},{7,8},{9,10},{11,12},{13,14},{15,16},{17,18},{19... | collective-permute-start | bytes 221192 | tf_op jit(solution)/shard_map/ppermute | solution.py:501
  7.7 2.6 %collective-permute-start.3 = (f32[224,128]{1,0:T(8,128)S(1)}, f32[224,128]{1,0:T(8,128)S(1)}, u32[]{:S(2)}, u32[]{:S(2)}) collective-permute-start(f32[224,128]{1,0:T(8,128)S(1)} %get-tuple-element.26.own.sent), channel_id=1, source_target_pairs={{0,96},{32,64},{64,32},{96,0},{128,224},{160,192},{192,160},{224,1... | collective-permute-start | bytes 344072 | tf_op jit(solution)/shard_map/ppermute | solution.py:521
  10.3 0.5 %collective-permute-start.2 = (f32[224,128]{1,0:T(8,128)S(1)}, f32[224,128]{1,0:T(8,128)S(1)}, u32[]{:S(2)}, u32[]{:S(2)}) collective-permute-start(f32[224,128]{1,0:T(8,128)S(1)} %get-tuple-element.26.own.sent), channel_id=1, source_target_pairs={{0,64},{32,96},{64,0},{96,32},{128,192},{160,224},{192,128},{224,1... | collective-permute-start | bytes 344072 | tf_op jit(solution)/shard_map/ppermute | solution.py:521
  10.8 0.0 collective-permute-done.rest_1_
  10.8 0.7 %collective-permute-start.1 = (f32[224,128]{1,0:T(8,128)S(1)}, f32[224,128]{1,0:T(8,128)S(1)}, u32[]{:S(2)}, u32[]{:S(2)}) collective-permute-start(f32[224,128]{1,0:T(8,128)S(1)} %get-tuple-element.26.own.sent), channel_id=1, source_target_pairs={{0,32},{32,0},{64,96},{96,64},{128,160},{160,128},{192,224},{224,1... | collective-permute-start | bytes 344072 | tf_op jit(solution)/shard_map/ppermute | solution.py:521
  11.5 0.0 collective-permute-start.4
  11.5 1.3 %collective-permute-done.4.rest_0_ = f32[8,2304]{1,0:T(8,128)S(1)} collective-permute-done((f32[8,2304]{1,0:T(8,128)S(1)}, f32[8,2304]{1,0:T(8,128)S(1)}, u32[]{:S(2)}, u32[]{:S(2)}) %collective-permute-start.4) | collective-permute-done | bytes 73760 | tf_op jit(solution)/shard_map/ppermute | solution.py:502
  12.8 1.1 %collective-permute-done.3.three = f32[224,128]{1,0:T(8,128)S(1)} collective-permute-done((f32[224,128]{1,0:T(8,128)S(1)}, f32[224,128]{1,0:T(8,128)S(1)}, u32[]{:S(2)}, u32[]{:S(2)}) %collective-permute-start.3) | collective-permute-done | bytes 114720 | tf_op jit(solution)/shard_map/ppermute | solution.py:521
  13.9 2.5 %collective-permute-done.2.two = f32[224,128]{1,0:T(8,128)S(1)} collective-permute-done((f32[224,128]{1,0:T(8,128)S(1)}, f32[224,128]{1,0:T(8,128)S(1)}, u32[]{:S(2)}, u32[]{:S(2)}) %collective-permute-start.2) | collective-permute-done | bytes 114720 | tf_op jit(solution)/shard_map/ppermute | solution.py:521
  16.4 0.0 collective-permute-done.1.one
  16.4 0.6 %shard_map.47 = f32[224,128]{1,0:T(8,128)S(1)} custom-call(f32[224,128]{1,0:T(8,128)S(1)} %get-tuple-element.26.own.sent, f32[224,128]{1,0:T(8,128)S(1)} %collective-permute-done.1.one, f32[224,128]{1,0:T(8,128)S(1)} %collective-permute-done.2.two, f32[224,128]{1,0:T(8,128)S(1)} %collective-permute-done.3.three, s32[16]{0:T(128)S(1)} %get-tuple-element.33.meta.rest_2_.rest_1_), custom_call_target="tpu_custom_call" | custom-call | flops 1000000 | bytes 1000000 | tf_op jit(solution)/shard_map/pallas_call | solution.py:483
  17.0 2.1 %collective-permute-start.5 = (f32[224,128]{1,0:T(8,128)S(1)}, f32[224,128]{1,0:T(8,128)S(1)}, u32[]{:S(2)}, u32[]{:S(2)}) collective-permute-start(f32[224,128]{1,0:T(8,128)S(1)} %shard_map.47), channel_id=1, source_target_pairs={{0,128},{32,160},{64,192},{96,224},{128,0},{160,32},{192,64},{224,... | collective-permute-start | bytes 344072 | tf_op jit(solution)/shard_map/ppermute | solution.py:528
  19.1 3.2 %shard_map.48.bulk = f32[4,16,2304]{2,1,0:T(8,128)S(1)} custom-call(f32[4,16,2304]{2,1,0:T(8,128)S(1)} %get-tuple-element.22.q.rest_0_, f32[9,16,2304]{2,1,0:T(8,128)S(1)} %get-tuple-element.23.metric, f32[8,2304]{1,0:T(8,128)S(1)} %collective-permute-done.4.rest_0_, f32[8,2304]{1,0:T(8,128)S(1)} %collective-permute-done.rest_1_, ...), custom_call_target="tpu_custom_call" | custom-call | flops 12000000 | bytes 12000000 | tf_op jit(solution)/shard_map/pallas_call | solution.py:483
  22.3 0.0 collective-permute-done.5.mate
  22.3 1.5 %shard_map.49 = (f32[4,16,2304]{2,1,0:T(8,128)S(1)}, f32[8,2432]{1,0:T(8,128)S(1)}, f32[8,2432]{1,0:T(8,128)S(1)}) custom-call(f32[4,16,2304]{2,1,0:T(8,128)S(1)} %shard_map.48.bulk, f32[4,16,2304]{2,1,0:T(8,128)S(1)} %get-tuple-element.22.q.rest_0_, f32[9,16,2304]{2,1,0:T(8,128)S(1)} %get-tuple-element.23.metric, ...), custom_call_target="tpu_custom_call" | custom-call | flops 1000000 | bytes 1000000 | tf_op jit(solution)/shard_map/pallas_call | solution.py:483
  23.8 0.1 collective-permute-start.6
  23.9 4.7 %collective-permute-start.7 = (f32[8,2432]{1,0:T(8,128)S(1)}, f32[8,2432]{1,0:T(8,128)S(1)}, u32[]{:S(2)}, u32[]{:S(2)}) collective-permute-start(f32[8,2432]{1,0:T(8,128)S(1)} %get-tuple-element.38), channel_id=1, source_target_pairs={{1,2},{3,4},{5,6},{7,8},{9,10},{11,12},{13,14},{15,16},{17,18},{19... | collective-permute-start | bytes 233480 | tf_op jit(solution)/shard_map/ppermute | solution.py:501
  28.6 3.2 %shard_map.50.part = f32[4,16,2304]{2,1,0:T(8,128)S(1)} custom-call(f32[4,16,2304]{2,1,0:T(8,128)S(1)} %get-tuple-element.36.q, f32[9,16,2304]{2,1,0:T(8,128)S(1)} %get-tuple-element.23.metric, f32[4,16,2304]{2,1,0:T(8,128)S(1)} %get-tuple-element.22.q.rest_0_, s32[16]{0:T(128)S(1)} %get-tuple-element.33.meta.rest_2_.rest_1_), custom_call_target="tpu_custom_call" | custom-call | flops 12000000 | bytes 12000000 | tf_op jit(solution)/shard_map/pallas_call | solution.py:483
  31.8 0.0 collective-permute-done.6.even_in
  31.8 0.0 collective-permute-done.7.odd_in
  31.8 2.6 %shard_map.51 = f32[4,16,2304]{2,1,0:T(8,128)} custom-call(f32[4,16,2304]{2,1,0:T(8,128)S(1)} %shard_map.50.part, f32[224,128]{1,0:T(8,128)S(1)} %get-tuple-element.26.own.sent, f32[4,16,2304]{2,1,0:T(8,128)S(1)} %get-tuple-element.36.q, f32[9,16,2304]{2,1,0:T(8,128)S(1)} %get-tuple-element.23.metric, f32[224,128]{1,0:T(8,128)S(1)} %collective-permute-done.1.one, ...), custom_call_target="tpu_custom_call" | custom-call | flops 1000000 | bytes 1000000 | tf_op jit(solution)/shard_map/pallas_call | solution.py:483
Async XLA Ops:
  2.5 8.3 %collective-permute-start = (f32[8,2304]{1,0:T(8,128)S(1)}, f32[8,2304]{1,0:T(8,128)S(1)}, u32[]{:S(2)}, u32[]{:S(2)}) collective-permute-start(f32[8,2304]{1,0:T(8,128)S(1)} %get-tuple-element.25), channel_id=1, source_target_pairs={{1,2},{3,4},{5,6},{7,8},{9,10},{11,12},{13,14},{15,16},{17,18},{19... | collective-permute-start | bytes 221192 | tf_op jit(solution)/shard_map/ppermute | solution.py:501
  7.7 6.2 %collective-permute-start.3 = (f32[224,128]{1,0:T(8,128)S(1)}, f32[224,128]{1,0:T(8,128)S(1)}, u32[]{:S(2)}, u32[]{:S(2)}) collective-permute-start(f32[224,128]{1,0:T(8,128)S(1)} %get-tuple-element.26.own.sent), channel_id=1, source_target_pairs={{0,96},{32,64},{64,32},{96,0},{128,224},{160,192},{192,160},{224,1... | collective-permute-start | bytes 344072 | tf_op jit(solution)/shard_map/ppermute | solution.py:521
  10.3 6.1 %collective-permute-start.2 = (f32[224,128]{1,0:T(8,128)S(1)}, f32[224,128]{1,0:T(8,128)S(1)}, u32[]{:S(2)}, u32[]{:S(2)}) collective-permute-start(f32[224,128]{1,0:T(8,128)S(1)} %get-tuple-element.26.own.sent), channel_id=1, source_target_pairs={{0,64},{32,96},{64,0},{96,32},{128,192},{160,224},{192,128},{224,1... | collective-permute-start | bytes 344072 | tf_op jit(solution)/shard_map/ppermute | solution.py:521
  10.8 5.6 %collective-permute-start.1 = (f32[224,128]{1,0:T(8,128)S(1)}, f32[224,128]{1,0:T(8,128)S(1)}, u32[]{:S(2)}, u32[]{:S(2)}) collective-permute-start(f32[224,128]{1,0:T(8,128)S(1)} %get-tuple-element.26.own.sent), channel_id=1, source_target_pairs={{0,32},{32,0},{64,96},{96,64},{128,160},{160,128},{192,224},{224,1... | collective-permute-start | bytes 344072 | tf_op jit(solution)/shard_map/ppermute | solution.py:521
  11.5 1.3 %collective-permute-start.4 = (f32[8,2304]{1,0:T(8,128)S(1)}, f32[8,2304]{1,0:T(8,128)S(1)}, u32[]{:S(2)}, u32[]{:S(2)}) collective-permute-start(f32[8,2304]{1,0:T(8,128)S(1)} %get-tuple-element.27), channel_id=1, source_target_pairs={{0,1},{1,0},{2,3},{3,2},{4,5},{5,4},{6,7},{7,6},{8,9},{9,8},{10,11... | collective-permute-start | bytes 221192 | tf_op jit(solution)/shard_map/ppermute | solution.py:502
  17.0 5.3 %collective-permute-start.5 = (f32[224,128]{1,0:T(8,128)S(1)}, f32[224,128]{1,0:T(8,128)S(1)}, u32[]{:S(2)}, u32[]{:S(2)}) collective-permute-start(f32[224,128]{1,0:T(8,128)S(1)} %shard_map.47), channel_id=1, source_target_pairs={{0,128},{32,160},{64,192},{96,224},{128,0},{160,32},{192,64},{224,... | collective-permute-start | bytes 344072 | tf_op jit(solution)/shard_map/ppermute | solution.py:528
  23.8 8.0 %collective-permute-start.6 = (f32[8,2432]{1,0:T(8,128)S(1)}, f32[8,2432]{1,0:T(8,128)S(1)}, u32[]{:S(2)}, u32[]{:S(2)}) collective-permute-start(f32[8,2432]{1,0:T(8,128)S(1)} %get-tuple-element.37), channel_id=1, source_target_pairs={{0,1},{1,0},{2,3},{3,2},{4,5},{5,4},{6,7},{7,6},{8,9},{9,8},{10,11... | collective-permute-start | bytes 233480 | tf_op jit(solution)/shard_map/ppermute | solution.py:502
  23.9 7.9 %collective-permute-start.7 = (f32[8,2432]{1,0:T(8,128)S(1)}, f32[8,2432]{1,0:T(8,128)S(1)}, u32[]{:S(2)}, u32[]{:S(2)}) collective-permute-start(f32[8,2432]{1,0:T(8,128)S(1)} %get-tuple-element.38), channel_id=1, source_target_pairs={{1,2},{3,4},{5,6},{7,8},{9,10},{11,12},{13,14},{15,16},{17,18},{19... | collective-permute-start | bytes 233480 | tf_op jit(solution)/shard_map/ppermute | solution.py:501
where the time goes:
time: 34.9 us; the launch traced here: 34.4 us
  starting transfers between devices  15.9 us (46%)
  Pallas kernels  13.5 us (39%)
  waiting for transfers between devices  4.89 us (14%)
    pallas_call x5, Pallas kernels, local(): pl.pallas_call(kernel, out_shape=shapes, in_specs=[VMEM] * (len(operands)...  11 us
    ppermute x2, starting transfers between devices, along_chain(): from_odd = lax.ppermute(odd, 'blk', pairs + [(b, a) for a, b in pairs])  9.91 us
    ppermute x3, starting transfers between devices, on_device(): lax.ppermute(value, 'seg', [(i, i ^ s) for i in range(SEGS)])  3.78 us
    ppermute x3, waiting for transfers between devices, on_device(): lax.ppermute(value, 'seg', [(i, i ^ s) for i in range(SEGS)])  3.62 us
    pallas_call x1, Pallas kernels, on_device(): pl.pallas_call(first_kernel, out_shape=[FIELD, f32((9, LEN, CELLS)), JOIN...  2.53 us
    ppermute x1, starting transfers between devices, on_device(): mate = lax.ppermute(picked, 'seg', [(i, i ^ 4) for i in range(SEGS)])  2.1 us
    ppermute x2, waiting for transfers between devices, along_chain(): lax.ppermute(even, 'blk', [(i, i ^ 1) for i in range(CHAIN)])  1.27 us
  transfers between devices with their start and end apart: 8, of which 3 were waited for; matrix products, arithmetic and copies ran while one was open for 0% of the time, Pallas kernels for 18%

commit v1 on v0

--- a/solution.py
+++ b/solution.py
@@ -8,7 +8,7 @@
 
 LEN, CROSS, CELLS, TILES = 16, 48, 2304, 18
 GROUP = 6
-GEOMETRY, BELOW, ABOVE, ROWS = 64, 208, 216, 224
+GEOMETRY, BELOW, ABOVE, ROWS = 64, 144, 152, 160
 USED, SPARE = 96, 32
 FACE, ALONG, ACROSS, POSITION, HAS_LOW, HAS_HIGH, OWN, MATE = 0, 1, 2, 3, 4, 5, 6, 9
 PARTS = ((0, BELOW), (BELOW, ABOVE), (ABOVE, ROWS))
@@ -90,7 +90,7 @@
 
 
 def first_kernel(
-    q_hbm, metric_hbm, map_hbm, links_hbm, q, metric, joint_ref, even_ref, odd_ref, meta, block_map, links, sem
+    q_hbm, metric_hbm, map_hbm, links_hbm, q, metric, joint_ref, even_ref, odd_ref, meta, block_map, links, edges, sem
 ):
     copies = [
         pltpu.make_async_copy(source, target, sem.at[n])
@@ -128,16 +128,10 @@
     lane = lanes_of(LEN)
     near, deep = face_source(face, across, 0), face_source(face, across, 2)
     below, above = face_source(low_face, low_across, 0), face_source(high_face, high_across, 0)
+    turned = lambda values: jnp.where(along == 1, reversed_rows(values), values)
+    face_q = [gather_face(lambda t: q[c, :, where(t)], near) for c in range(4)]
     deeper = [gather_face(lambda t: q[c, :, where(t)], deep) for c in range(4)]
-
-    def put(n, values):
-        if n < 12:
-            third = pltpu.roll(deeper[n // 3], USED - SPARE * (n % 3), 1)
-            values = jnp.where(lane < USED, values, third)
-        joint_ref[LEN * n : LEN * n + LEN, :] = jnp.where(along == 1, reversed_rows(values), values)
-
-    for c in range(4):
-        put(c, gather_face(lambda t: q[c, :, where(t)], near))
+    for c in range(4):
         low_rows = gather_face(lambda t: q[c, 0:8, where(t)], below)
         joint_ref[BELOW + 2 * c : BELOW + 2 * c + 2, :] = low_rows[0:2]
         high_rows = gather_face(lambda t: q[c, 8:16, where(t)], above)
@@ -147,10 +141,64 @@
     inward = jnp.where((face == 3) | (face == 5), -1.0, 1.0)
     forward = jnp.where(along == 1, -1.0, 1.0)
     sideways = jnp.where(across == 1, -1.0, 1.0)
-    for a, (row, sign) in enumerate(((0, forward), (3 * normal, inward), (3 * (3 - normal), sideways))):
+    geometry = []
+    for row, sign in ((0, 1.0), (3 * normal, inward), (3 * (3 - normal), sideways)):
         for b in range(3):
-            found = gather_face(lambda t: metric[row + b, :, where(t)], near)
-            put(4 + 3 * a + b, sign * found)
+            geometry.append(sign * gather_face(lambda t: metric[row + b, :, where(t)], near))
+    part = own_face(face_q, deeper, geometry, meta)
+    edges[...] = jnp.zeros((LEN, 128), jnp.float32)
+    for n in range(3):
+        values = forward * turned(geometry[n])
+        edges[4 * n : 4 * n + 2, :] = values[0:2]
+        edges[4 * n + 2 : 4 * n + 4, :] = values[14:16]
+    packed = (turned(part[2]), turned(part[3]), edges[...])
+    for n, values in enumerate(face_q + geometry[3:6] + part[:2]):
+        third = pltpu.roll(packed[n // 3], USED - SPARE * (n % 3), 1)
+        joint_ref[LEN * n : LEN * n + LEN, :] = jnp.where(lane < USED, turned(values), third)
+
+
+def unpacked(main, n):
+    lane = lanes_of(LEN)
+    thirds = [
+        pltpu.roll(main[LEN * (3 * n + h) : LEN * (3 * n + h) + LEN, :], (SPARE * h - USED) % 128, 1) for h in range(3)
+    ]
+    return jnp.where(lane < SPARE, thirds[0], jnp.where(lane < 2 * SPARE, thirds[1], thirds[2]))
+
+
+def own_face(face_q, deeper, geometry, meta):
+    lane = lanes_of(LEN)
+    row = lax.broadcasted_iota(jnp.int32, (8, 128), 0)
+    place = jnp.where(lane >= CROSS, lane - CROSS, lane)
+    outer = lane < CROSS
+    open_low = jnp.where(meta[HAS_LOW] == 0, 1.0, 0.0)
+    open_high = jnp.where(meta[HAS_HIGH] == 0, 1.0, 0.0)
+    stencils = []
+    for c in range(4):
+        here, deep = face_q[c], deeper[c]
+        top, bottom = here[0:8], here[8:16]
+        low = -SIGN[c] * open_low * jnp.where(row == 7, pltpu.roll(top, 7, 0), pltpu.roll(top, 5, 0))
+        high = -SIGN[c] * open_high * jnp.where(row == 0, pltpu.roll(bottom, 1, 0), pltpu.roll(bottom, 3, 0))
+        rows = jnp.concatenate([low, here, high], axis=0)
+        along_i = [shifted_rows(rows, s) for s in (-2, -1)] + [here] + [shifted_rows(rows, s) for s in (1, 2)]
+        normal = [
+            jnp.zeros((LEN, 128), jnp.float32),
+            jnp.where(outer, 0.0, pltpu.roll(here, 48, 1)),
+            here,
+            jnp.where(outer, pltpu.roll(here, 80, 1), pltpu.roll(deep, 48, 1)),
+            deep,
+        ]
+        raw = [pltpu.roll(here, (-s) % 128, 1) if s else here for s in range(-2, 3)]
+        wall = SIGN[c] * here
+        second = SIGN[c] * jnp.where((place == 0) | (place == 46), raw[3], raw[1])
+        sideways = [
+            jnp.where(place < 2, second, raw[0]),
+            jnp.where(place == 0, wall, raw[1]),
+            here,
+            jnp.where(place == 47, wall, raw[3]),
+            jnp.where(place >= 46, second, raw[4]),
+        ]
+        stencils.append((along_i, normal, sideways))
+    return advance(stencils, geometry)
 
 
 def copy_part(choice, refs, rows, out):
@@ -297,67 +345,69 @@
     return added
 
 
-def partner_face(sent, main, low_ref, high_ref, from_low, from_high, meta, ghost_ref):
+def partner_face(sent, main, ends_ref, from_low, from_high, meta, ghost_ref):
     lane = lanes_of(LEN)
-    place = jnp.where(lane >= CROSS, lane - CROSS, lane)
+    row = lax.broadcasted_iota(jnp.int32, (8, 128), 0)
     along, across = meta[ALONG] == 1, meta[ACROSS] == 1
-    missing_low = jnp.where(along, meta[HAS_HIGH], meta[HAS_LOW]) == 0
-    missing_high = jnp.where(along, meta[HAS_LOW], meta[HAS_HIGH]) == 0
+    has_low = jnp.where(jnp.where(along, meta[HAS_HIGH], meta[HAS_LOW]) == 1, 1.0, 0.0)
+    has_high = jnp.where(jnp.where(along, meta[HAS_LOW], meta[HAS_HIGH]) == 1, 1.0, 0.0)
     mirrored = jnp.where(lane < CROSS, CROSS - 1 - lane, jnp.where(lane < 2 * CROSS, 3 * CROSS - 1 - lane, lane))[:8]
-    stencils = []
+    rows_of = lambda n: main[LEN * n : LEN * n + LEN, :]
+    here = [rows_of(c) for c in range(4)]
+    slopes, curves = [], []
     for c in range(4):
         mine = sent[LEN * c : LEN * c + LEN, :]
         mine = jnp.where(across, gather_lanes(mine, mirrored), mine)
         mine = jnp.where(along, reversed_rows(mine), mine)
-        here = main[LEN * c : LEN * c + LEN, :]
-        thirds = [
-            pltpu.roll(main[LEN * n : LEN * n + LEN, :], (SPARE * (n % 3) - USED) % 128, 1) for n in range(3 * c, 3 * c + 3)
-        ]
-        deep = jnp.where(lane < SPARE, thirds[0], jnp.where(lane < 2 * SPARE, thirds[1], thirds[2]))
+        first = jnp.where(lane < CROSS, mine, 0.0)
+        second = jnp.where(lane < CROSS, pltpu.roll(mine, 80, 1), pltpu.roll(mine, 48, 1))
+        second = jnp.where(lane < 2 * CROSS, second, 0.0)
+        slopes.append(second - 8.0 * first)
+        curves.append(16.0 * first - second)
+    added = edge_terms(here, [rows_of(4 + n) for n in range(3)], slopes, curves, 1.0)
+    parts = [rows_of(7), rows_of(8), unpacked(main, 0), unpacked(main, 1)]
+
+    ends_ref[...] = jnp.zeros((7, 8, 128), jnp.float32)
+    metric_ends = unpacked(main, 2)
+    for n in range(3):
+        ends_ref[4 + n, 0:2, :] = metric_ends[4 * n : 4 * n + 2]
+        ends_ref[4 + n, 6:8, :] = metric_ends[4 * n + 2 : 4 * n + 4]
+    for c in range(4):
         below, above = from_low[2 * c : 2 * c + 2, :], from_high[2 * c : 2 * c + 2, :]
-        low_ref[6:7, :] = jnp.where(missing_low, -SIGN[c] * here[1:2], jnp.where(along, above[1:2], below[0:1]))
-        low_ref[7:8, :] = jnp.where(missing_low, -SIGN[c] * here[0:1], jnp.where(along, above[0:1], below[1:2]))
-        high_ref[0:1, :] = jnp.where(missing_high, -SIGN[c] * here[15:16], jnp.where(along, below[1:2], above[0:1]))
-        high_ref[1:2, :] = jnp.where(missing_high, -SIGN[c] * here[14:15], jnp.where(along, below[0:1], above[1:2]))
-        rows = jnp.concatenate([low_ref[...], here, high_ref[...]], axis=0)
-        along_i = [shifted_rows(rows, s) for s in (-2, -1)] + [here] + [shifted_rows(rows, s) for s in (1, 2)]
-        outer = lane < CROSS
-        normal = [
-            jnp.where(outer, pltpu.roll(mine, 80, 1), pltpu.roll(mine, 48, 1)),
-            jnp.where(outer, mine, pltpu.roll(here, 48, 1)),
-            here,
-            jnp.where(outer, pltpu.roll(here, 80, 1), pltpu.roll(deep, 48, 1)),
-            deep,
-        ]
-        raw = [pltpu.roll(here, (-s) % 128, 1) if s else here for s in range(-2, 3)]
-        wall = SIGN[c] * here
-        second = SIGN[c] * jnp.where((place == 0) | (place == 46), raw[3], raw[1])
-        sideways = [
-            jnp.where(place < 2, second, raw[0]),
-            jnp.where(place == 0, wall, raw[1]),
-            here,
-            jnp.where(place == 47, wall, raw[3]),
-            jnp.where(place >= 46, second, raw[4]),
-        ]
-        stencils.append((along_i, normal, sideways))
-    geometry = [main[GEOMETRY + LEN * n : GEOMETRY + LEN * n + LEN, :] for n in range(9)]
-    for c, values in enumerate(advance(stencils, geometry)):
-        ghost_ref[LEN * c : LEN * c + LEN, :] = values
+        ends_ref[c, 0:1, :] = has_low * jnp.where(along, above[1:2], below[0:1])
+        ends_ref[c, 1:2, :] = has_low * jnp.where(along, above[0:1], below[1:2])
+        ends_ref[c, 6:7, :] = has_high * jnp.where(along, below[1:2], above[0:1])
+        ends_ref[c, 7:8, :] = has_high * jnp.where(along, below[0:1], above[1:2])
+    slopes, curves = [], []
+    for c in range(4):
+        slope, curve = chain_stencil(ends_ref[c], row)
+        slopes.append(slope)
+        curves.append(curve)
+    start = row < 4
+    at_ends = [jnp.where(start, here[c][0:8], here[c][8:16]) for c in range(4)]
+    more = edge_terms(at_ends, [ends_ref[4 + n] for n in range(3)], slopes, curves, 1.0)
+    for c in range(4):
+        values = parts[c] + added[c]
+        ghost_ref[LEN * c : LEN * c + 8, :] = values[0:8] + jnp.where(start, more[c], 0.0)
+        ghost_ref[LEN * c + 8 : LEN * c + LEN, :] = values[8:16] + jnp.where(start, 0.0, more[c])
+
+
+def chain_stencil(second, row):
+    first = jnp.where(row == 0, pltpu.roll(second, 7, 0), jnp.where(row == 7, pltpu.roll(second, 1, 0), 0.0))
+    return jnp.where(row < 4, -1.0, 1.0) * (8.0 * first - second), 16.0 * first - second
 
 
 def chain_terms(q, metric, chain_ref, scale, tiles, base, out):
     row = lax.broadcasted_iota(jnp.int32, (8, 128), 0)
     start = row < 4
-    toward = jnp.where(start, -1.0, 1.0)
     for t in tiles:
         where = slice(128 * t, 128 * t + 128)
         ends = lambda ref, n: jnp.where(start, ref[n, 0:8, where], ref[n, 8:16, where])
         slopes, curves = [], []
         for c in range(4):
-            second = chain_ref[c, :, where]
-            first = jnp.where(row == 0, pltpu.roll(second, 7, 0), jnp.where(row == 7, pltpu.roll(second, 1, 0), 0.0))
-            slopes.append(toward * (8.0 * first - second))
-            curves.append(16.0 * first - second)
+            slope, curve = chain_stencil(chain_ref[c, :, where], row)
+            slopes.append(slope)
+            curves.append(curve)
         added = edge_terms([ends(q, c) for c in range(4)], [ends(metric, n) for n in range(3)], slopes, curves, scale)
         for c in range(4):
             out[c, 0:8, where] = base[c, 0:8, where] + jnp.where(start, added[c], 0.0)
@@ -449,13 +499,13 @@
 
 
 def last_kernel(part, sent, q, metric, one, two, three, mate, even_in, odd_in, meta, out_hbm, *scratch):
-    chain_ref, ghost_ref, main, first_low, first_high, out, sem = scratch
+    chain_ref, ghost_ref, main, ends_ref, out, sem = scratch
     even = lax.rem(meta[POSITION], 2) == 0
     copy_part(meta[OWN], (mate, one, two, three), PARTS[0], main)
     spare = slice(CELLS, CELLS + 128)
     from_even, from_odd = even_in[:, spare], odd_in[:, spare]
     from_low, from_high = jnp.where(even, from_odd, from_even), jnp.where(even, from_even, from_odd)
-    partner_face(sent, main, first_low, first_high, from_low, from_high, meta, ghost_ref)
+    partner_face(sent, main, ends_ref, from_low, from_high, meta, ghost_ref)
     spread_ghosts(even_in, odd_in, meta, chain_ref)
     copies = []
     for n in range(TILES // GROUP):
@@ -514,6 +564,7 @@
         scratch_shapes=[
             pltpu.SMEM((SEGS * CHAIN,), jnp.int32),
             pltpu.SMEM((6, 4, SEGS * CHAIN), jnp.int32),
+            pltpu.VMEM((LEN, 128), jnp.float32),
             pltpu.SemaphoreType.DMA((4,)),
         ],
         compiler_params=PARAMS,
@@ -540,7 +591,7 @@
         last_kernel,
         [FIELD],
         (part, joint, q1, geometry, one, two, three, mate, from_even, from_odd, meta),
-        [CHAIN_TILES, GHOST, pltpu.VMEM((BELOW, 128), jnp.float32), TILE, TILE]
+        [CHAIN_TILES, GHOST, pltpu.VMEM((BELOW, 128), jnp.float32), pltpu.VMEM((7, 8, 128), jnp.float32)]
         + [pltpu.VMEM((4, LEN, CELLS), jnp.float32), pltpu.SemaphoreType.DMA((TILES // GROUP,))],
         out_specs=[HBM],
     )

time: 34.9 us -> 33.8 us (0.968)
  the two profiles are of different devices: /device:TPU:105 before, /device:TPU:111 now
where the time goes in v1:
time: 33.8 us; the launch traced here: 33.6 us
  starting transfers between devices  17 us (50%)
  Pallas kernels  12 us (36%)
  waiting for transfers between devices  4.48 us (13%)
    ppermute x2, starting transfers between devices, along_chain(): from_odd = lax.ppermute(odd, 'blk', pairs + [(b, a) for a, b in pairs])  11.6 us
    pallas_call x5, Pallas kernels, local(): pl.pallas_call(kernel, out_shape=shapes, in_specs=[VMEM] * (len(operands)...  9.52 us
    ppermute x3, starting transfers between devices, on_device(): lax.ppermute(value, 'seg', [(i, i ^ s) for i in range(SEGS)])  2.9 us
    pallas_call x1, Pallas kernels, on_device(): pl.pallas_call(first_kernel, out_shape=[FIELD, f32((9, LEN, CELLS)), JOIN...  2.52 us
    ppermute x1, starting transfers between devices, on_device(): mate = lax.ppermute(picked, 'seg', [(i, i ^ 4) for i in range(SEGS)])  2.1 us
    ppermute x3, waiting for transfers between devices, on_device(): lax.ppermute(value, 'seg', [(i, i ^ s) for i in range(SEGS)])  2.03 us
    ppermute x2, waiting for transfers between devices, along_chain(): lax.ppermute(even, 'blk', [(i, i ^ 1) for i in range(CHAIN)])  1.27 us
    ppermute x1, waiting for transfers between devices, on_device(): mate = lax.ppermute(picked, 'seg', [(i, i ^ 4) for i in range(SEGS)])  0.74 us
  transfers between devices with their start and end apart: 8, of which 6 were waited for; matrix products, arithmetic and copies ran while one was open for 0% of the time, Pallas kernels for 19%

profile of v1, /device:TPU:111, one launch (start us, length us, event | category | flops | bytes accessed | tf_op | source)
XLA Modules:
  0.0 33.6 jit_solution(1743036170452138439)
XLA Ops:
  0.0 2.5 %shard_map.46 = (f32[4,16,2304]{2,1,0:T(8,128)S(1)}, f32[9,16,2304]{2,1,0:T(8,128)S(1)}, f32[160,128]{1,0:T(8,128)S(1)}, f32[8,2304]{1,0:T(8,128)S(1)}, f32[8,2304]{1,0:T(8,128)S(1)}, /*index=5*/s32[16]{0:T(128)S(1)}) custom-call(f32[4,16,2304]{2,1,0:T(8,128)} %bitcast.5, f32[9,16,2304]{2,1,0:T(8,128)} %bitcast.4, s32[256]{0:T(256)} %map_hbm.1, ...), custom_call_target="tpu_custom_call" | custom-call | tf_op jit(solution)/shard_map/pallas_call | solution.py:559
  2.5 5.2 %collective-permute-start = (f32[8,2304]{1,0:T(8,128)S(1)}, f32[8,2304]{1,0:T(8,128)S(1)}, u32[]{:S(2)}, u32[]{:S(2)}) collective-permute-start(f32[8,2304]{1,0:T(8,128)S(1)} %get-tuple-element.25), channel_id=1, source_target_pairs={{1,2},{3,4},{5,6},{7,8},{9,10},{11,12},{13,14},{15,16},{17,18},{19... | collective-permute-start | bytes 221192 | tf_op jit(solution)/shard_map/ppermute | solution.py:551
  7.7 0.3 collective-permute-start.3
  8.0 2.1 %collective-permute-start.2 = (f32[160,128]{1,0:T(8,128)S(1)}, f32[160,128]{1,0:T(8,128)S(1)}, u32[]{:S(2)}, u32[]{:S(2)}) collective-permute-start(f32[160,128]{1,0:T(8,128)S(1)} %get-tuple-element.26.own.sent), channel_id=1, source_target_pairs={{0,64},{32,96},{64,0},{96,32},{128,192},{160,224},{192,128},{224,1... | collective-permute-start | bytes 245768 | tf_op jit(solution)/shard_map/ppermute | solution.py:572
  10.2 0.4 %collective-permute-done.rest_1_ = f32[8,2304]{1,0:T(8,128)S(1)} collective-permute-done((f32[8,2304]{1,0:T(8,128)S(1)}, f32[8,2304]{1,0:T(8,128)S(1)}, u32[]{:S(2)}, u32[]{:S(2)}) %collective-permute-start) | collective-permute-done | bytes 73760 | tf_op jit(solution)/shard_map/ppermute | solution.py:551
  10.6 0.5 %collective-permute-start.1 = (f32[160,128]{1,0:T(8,128)S(1)}, f32[160,128]{1,0:T(8,128)S(1)}, u32[]{:S(2)}, u32[]{:S(2)}) collective-permute-start(f32[160,128]{1,0:T(8,128)S(1)} %get-tuple-element.26.own.sent), channel_id=1, source_target_pairs={{0,32},{32,0},{64,96},{96,64},{128,160},{160,128},{192,224},{224,1... | collective-permute-start | bytes 245768 | tf_op jit(solution)/shard_map/ppermute | solution.py:572
  11.1 0.0 collective-permute-start.4
  11.1 1.3 %collective-permute-done.4.rest_0_ = f32[8,2304]{1,0:T(8,128)S(1)} collective-permute-done((f32[8,2304]{1,0:T(8,128)S(1)}, f32[8,2304]{1,0:T(8,128)S(1)}, u32[]{:S(2)}, u32[]{:S(2)}) %collective-permute-start.4) | collective-permute-done | bytes 73760 | tf_op jit(solution)/shard_map/ppermute | solution.py:552
  12.3 0.4 %collective-permute-done.3.three = f32[160,128]{1,0:T(8,128)S(1)} collective-permute-done((f32[160,128]{1,0:T(8,128)S(1)}, f32[160,128]{1,0:T(8,128)S(1)}, u32[]{:S(2)}, u32[]{:S(2)}) %collective-permute-start.3) | collective-permute-done | bytes 81952 | tf_op jit(solution)/shard_map/ppermute | solution.py:572
  12.7 0.7 %collective-permute-done.2.two = f32[160,128]{1,0:T(8,128)S(1)} collective-permute-done((f32[160,128]{1,0:T(8,128)S(1)}, f32[160,128]{1,0:T(8,128)S(1)}, u32[]{:S(2)}, u32[]{:S(2)}) %collective-permute-start.2) | collective-permute-done | bytes 81952 | tf_op jit(solution)/shard_map/ppermute | solution.py:572
  13.4 1.0 %collective-permute-done.1.one = f32[160,128]{1,0:T(8,128)S(1)} collective-permute-done((f32[160,128]{1,0:T(8,128)S(1)}, f32[160,128]{1,0:T(8,128)S(1)}, u32[]{:S(2)}, u32[]{:S(2)}) %collective-permute-start.1) | collective-permute-done | bytes 81952 | tf_op jit(solution)/shard_map/ppermute | solution.py:572
  14.4 0.6 %shard_map.47 = f32[160,128]{1,0:T(8,128)S(1)} custom-call(f32[160,128]{1,0:T(8,128)S(1)} %get-tuple-element.26.own.sent, f32[160,128]{1,0:T(8,128)S(1)} %collective-permute-done.1.one, f32[160,128]{1,0:T(8,128)S(1)} %collective-permute-done.2.two, f32[160,128]{1,0:T(8,128)S(1)} %collective-permute-done.3.three, s32[16]{0:T(128)S(1)} %get-tuple-element.33.meta.rest_2_.rest_1_), custom_call_target="tpu_custom_call" | custom-call | flops 1000000 | bytes 1000000 | tf_op jit(solution)/shard_map/pallas_call | solution.py:533
  15.0 2.1 %collective-permute-start.5 = (f32[160,128]{1,0:T(8,128)S(1)}, f32[160,128]{1,0:T(8,128)S(1)}, u32[]{:S(2)}, u32[]{:S(2)}) collective-permute-start(f32[160,128]{1,0:T(8,128)S(1)} %shard_map.47), channel_id=1, source_target_pairs={{0,128},{32,160},{64,192},{96,224},{128,0},{160,32},{192,64},{224,... | collective-permute-start | bytes 245768 | tf_op jit(solution)/shard_map/ppermute | solution.py:579
  17.1 3.2 %shard_map.48.bulk = f32[4,16,2304]{2,1,0:T(8,128)S(1)} custom-call(f32[4,16,2304]{2,1,0:T(8,128)S(1)} %get-tuple-element.22.q.rest_0_, f32[9,16,2304]{2,1,0:T(8,128)S(1)} %get-tuple-element.23.metric, f32[8,2304]{1,0:T(8,128)S(1)} %collective-permute-done.4.rest_0_, f32[8,2304]{1,0:T(8,128)S(1)} %collective-permute-done.rest_1_, ...), custom_call_target="tpu_custom_call" | custom-call | flops 12000000 | bytes 12000000 | tf_op jit(solution)/shard_map/pallas_call | solution.py:533
  20.3 0.7 %collective-permute-done.5.mate = f32[160,128]{1,0:T(8,128)S(1)} collective-permute-done((f32[160,128]{1,0:T(8,128)S(1)}, f32[160,128]{1,0:T(8,128)S(1)}, u32[]{:S(2)}, u32[]{:S(2)}) %collective-permute-start.5) | collective-permute-done | bytes 81952 | tf_op jit(solution)/shard_map/ppermute | solution.py:579
  21.0 0.8 %shard_map.49 = (f32[4,16,2304]{2,1,0:T(8,128)S(1)}, f32[8,2432]{1,0:T(8,128)S(1)}, f32[8,2432]{1,0:T(8,128)S(1)}) custom-call(f32[4,16,2304]{2,1,0:T(8,128)S(1)} %shard_map.48.bulk, f32[4,16,2304]{2,1,0:T(8,128)S(1)} %get-tuple-element.22.q.rest_0_, f32[9,16,2304]{2,1,0:T(8,128)S(1)} %get-tuple-element.23.metric, ...), custom_call_target="tpu_custom_call" | custom-call | flops 1000000 | bytes 1000000 | tf_op jit(solution)/shard_map/pallas_call | solution.py:533
  21.8 0.4 %collective-permute-start.6 = (f32[8,2432]{1,0:T(8,128)S(1)}, f32[8,2432]{1,0:T(8,128)S(1)}, u32[]{:S(2)}, u32[]{:S(2)}) collective-permute-start(f32[8,2432]{1,0:T(8,128)S(1)} %get-tuple-element.37), channel_id=1, source_target_pairs={{0,1},{1,0},{2,3},{3,2},{4,5},{5,4},{6,7},{7,6},{8,9},{9,8},{10,11... | collective-permute-start | bytes 233480 | tf_op jit(solution)/shard_map/ppermute | solution.py:552
  22.2 6.4 %collective-permute-start.7 = (f32[8,2432]{1,0:T(8,128)S(1)}, f32[8,2432]{1,0:T(8,128)S(1)}, u32[]{:S(2)}, u32[]{:S(2)}) collective-permute-start(f32[8,2432]{1,0:T(8,128)S(1)} %get-tuple-element.38), channel_id=1, source_target_pairs={{1,2},{3,4},{5,6},{7,8},{9,10},{11,12},{13,14},{15,16},{17,18},{19... | collective-permute-start | bytes 233480 | tf_op jit(solution)/shard_map/ppermute | solution.py:551
  28.6 3.2 %shard_map.50.part = f32[4,16,2304]{2,1,0:T(8,128)S(1)} custom-call(f32[4,16,2304]{2,1,0:T(8,128)S(1)} %get-tuple-element.36.q, f32[9,16,2304]{2,1,0:T(8,128)S(1)} %get-tuple-element.23.metric, f32[4,16,2304]{2,1,0:T(8,128)S(1)} %get-tuple-element.22.q.rest_0_, s32[16]{0:T(128)S(1)} %get-tuple-element.33.meta.rest_2_.rest_1_), custom_call_target="tpu_custom_call" | custom-call | flops 12000000 | bytes 12000000 | tf_op jit(solution)/shard_map/pallas_call | solution.py:533
  31.8 0.0 collective-permute-done.6.even_in
  31.8 0.0 collective-permute-done.7.odd_in
  31.8 1.8 %shard_map.51 = f32[4,16,2304]{2,1,0:T(8,128)} custom-call(f32[4,16,2304]{2,1,0:T(8,128)S(1)} %shard_map.50.part, f32[160,128]{1,0:T(8,128)S(1)} %get-tuple-element.26.own.sent, f32[4,16,2304]{2,1,0:T(8,128)S(1)} %get-tuple-element.36.q, f32[9,16,2304]{2,1,0:T(8,128)S(1)} %get-tuple-element.23.metric, f32[160,128]{1,0:T(8,128)S(1)} %collective-permute-done.1.one, ...), custom_call_target="tpu_custom_call" | custom-call | flops 1000000 | bytes 1000000 | tf_op jit(solution)/shard_map/pallas_call | solution.py:533
Async XLA Ops:
  2.5 8.1 %collective-permute-start = (f32[8,2304]{1,0:T(8,128)S(1)}, f32[8,2304]{1,0:T(8,128)S(1)}, u32[]{:S(2)}, u32[]{:S(2)}) collective-permute-start(f32[8,2304]{1,0:T(8,128)S(1)} %get-tuple-element.25), channel_id=1, source_target_pairs={{1,2},{3,4},{5,6},{7,8},{9,10},{11,12},{13,14},{15,16},{17,18},{19... | collective-permute-start | bytes 221192 | tf_op jit(solution)/shard_map/ppermute | solution.py:551
  7.7 5.0 %collective-permute-start.3 = (f32[160,128]{1,0:T(8,128)S(1)}, f32[160,128]{1,0:T(8,128)S(1)}, u32[]{:S(2)}, u32[]{:S(2)}) collective-permute-start(f32[160,128]{1,0:T(8,128)S(1)} %get-tuple-element.26.own.sent), channel_id=1, source_target_pairs={{0,96},{32,64},{64,32},{96,0},{128,224},{160,192},{192,160},{224,1... | collective-permute-start | bytes 245768 | tf_op jit(solution)/shard_map/ppermute | solution.py:572
  8.0 5.4 %collective-permute-start.2 = (f32[160,128]{1,0:T(8,128)S(1)}, f32[160,128]{1,0:T(8,128)S(1)}, u32[]{:S(2)}, u32[]{:S(2)}) collective-permute-start(f32[160,128]{1,0:T(8,128)S(1)} %get-tuple-element.26.own.sent), channel_id=1, source_target_pairs={{0,64},{32,96},{64,0},{96,32},{128,192},{160,224},{192,128},{224,1... | collective-permute-start | bytes 245768 | tf_op jit(solution)/shard_map/ppermute | solution.py:572
  10.6 3.8 %collective-permute-start.1 = (f32[160,128]{1,0:T(8,128)S(1)}, f32[160,128]{1,0:T(8,128)S(1)}, u32[]{:S(2)}, u32[]{:S(2)}) collective-permute-start(f32[160,128]{1,0:T(8,128)S(1)} %get-tuple-element.26.own.sent), channel_id=1, source_target_pairs={{0,32},{32,0},{64,96},{96,64},{128,160},{160,128},{192,224},{224,1... | collective-permute-start | bytes 245768 | tf_op jit(solution)/shard_map/ppermute | solution.py:572
  11.1 1.3 %collective-permute-start.4 = (f32[8,2304]{1,0:T(8,128)S(1)}, f32[8,2304]{1,0:T(8,128)S(1)}, u32[]{:S(2)}, u32[]{:S(2)}) collective-permute-start(f32[8,2304]{1,0:T(8,128)S(1)} %get-tuple-element.27), channel_id=1, source_target_pairs={{0,1},{1,0},{2,3},{3,2},{4,5},{5,4},{6,7},{7,6},{8,9},{9,8},{10,11... | collective-permute-start | bytes 221192 | tf_op jit(solution)/shard_map/ppermute | solution.py:552
  15.0 6.0 %collective-permute-start.5 = (f32[160,128]{1,0:T(8,128)S(1)}, f32[160,128]{1,0:T(8,128)S(1)}, u32[]{:S(2)}, u32[]{:S(2)}) collective-permute-start(f32[160,128]{1,0:T(8,128)S(1)} %shard_map.47), channel_id=1, source_target_pairs={{0,128},{32,160},{64,192},{96,224},{128,0},{160,32},{192,64},{224,... | collective-permute-start | bytes 245768 | tf_op jit(solution)/shard_map/ppermute | solution.py:579
  21.8 10.0 %collective-permute-start.6 = (f32[8,2432]{1,0:T(8,128)S(1)}, f32[8,2432]{1,0:T(8,128)S(1)}, u32[]{:S(2)}, u32[]{:S(2)}) collective-permute-start(f32[8,2432]{1,0:T(8,128)S(1)} %get-tuple-element.37), channel_id=1, source_target_pairs={{0,1},{1,0},{2,3},{3,2},{4,5},{5,4},{6,7},{7,6},{8,9},{9,8},{10,11... | collective-permute-start | bytes 233480 | tf_op jit(solution)/shard_map/ppermute | solution.py:552
  22.2 9.6 %collective-permute-start.7 = (f32[8,2432]{1,0:T(8,128)S(1)}, f32[8,2432]{1,0:T(8,128)S(1)}, u32[]{:S(2)}, u32[]{:S(2)}) collective-permute-start(f32[8,2432]{1,0:T(8,128)S(1)} %get-tuple-element.38), channel_id=1, source_target_pairs={{1,2},{3,4},{5,6},{7,8},{9,10},{11,12},{13,14},{15,16},{17,18},{19... | collective-permute-start | bytes 233480 | tf_op jit(solution)/shard_map/ppermute | solution.py:551

commit v2 on v1

--- a/solution.py
+++ b/solution.py
@@ -346,24 +346,17 @@
 
 
 def partner_face(sent, main, ends_ref, from_low, from_high, meta, ghost_ref):
-    lane = lanes_of(LEN)
     row = lax.broadcasted_iota(jnp.int32, (8, 128), 0)
-    along, across = meta[ALONG] == 1, meta[ACROSS] == 1
+    along = meta[ALONG] == 1
     has_low = jnp.where(jnp.where(along, meta[HAS_HIGH], meta[HAS_LOW]) == 1, 1.0, 0.0)
     has_high = jnp.where(jnp.where(along, meta[HAS_LOW], meta[HAS_HIGH]) == 1, 1.0, 0.0)
-    mirrored = jnp.where(lane < CROSS, CROSS - 1 - lane, jnp.where(lane < 2 * CROSS, 3 * CROSS - 1 - lane, lane))[:8]
     rows_of = lambda n: main[LEN * n : LEN * n + LEN, :]
     here = [rows_of(c) for c in range(4)]
     slopes, curves = [], []
     for c in range(4):
-        mine = sent[LEN * c : LEN * c + LEN, :]
-        mine = jnp.where(across, gather_lanes(mine, mirrored), mine)
-        mine = jnp.where(along, reversed_rows(mine), mine)
-        first = jnp.where(lane < CROSS, mine, 0.0)
-        second = jnp.where(lane < CROSS, pltpu.roll(mine, 80, 1), pltpu.roll(mine, 48, 1))
-        second = jnp.where(lane < 2 * CROSS, second, 0.0)
-        slopes.append(second - 8.0 * first)
-        curves.append(16.0 * first - second)
+        slope, curve = face_stencil(turned_back(sent[LEN * c : LEN * c + LEN, :], meta))
+        slopes.append(slope)
+        curves.append(curve)
     added = edge_terms(here, [rows_of(4 + n) for n in range(3)], slopes, curves, 1.0)
     parts = [rows_of(7), rows_of(8), unpacked(main, 0), unpacked(main, 1)]
 
@@ -472,13 +465,59 @@
             add(t, 2, slopes, curves)
 
 
-def joint_kernel(bulk, q, metric, one, two, three, mate, meta, out, even_ref, odd_ref, ghost_ref, below, above):
+def turned_back(values, meta):
+    lane = lanes_of()
+    mirrored = jnp.where(lane < CROSS, CROSS - 1 - lane, jnp.where(lane < 2 * CROSS, 3 * CROSS - 1 - lane, lane))
+    values = jnp.where(meta[ACROSS] == 1, gather_lanes(values, mirrored), values)
+    return jnp.where(meta[ALONG] == 1, reversed_rows(values), values)
+
+
+def face_stencil(ghost):
+    lane = lanes_of(LEN)
+    first = jnp.where(lane < CROSS, ghost, 0.0)
+    second = jnp.where(lane < CROSS, pltpu.roll(ghost, 80, 1), pltpu.roll(ghost, 48, 1))
+    second = jnp.where(lane < 2 * CROSS, second, 0.0)
+    return second - 8.0 * first, 16.0 * first - second
+
+
+def joint_kernel(bulk, sent, one, two, three, mate, meta, out, even_ref, odd_ref, ghost_ref, below, above):
     received = (mate, one, two, three)
     copy_part(meta[OWN], received, (0, GEOMETRY), ghost_ref)
     copy_part(meta[OWN + 1], received, PARTS[1], below)
     copy_part(meta[OWN + 2], received, PARTS[2], above)
     out[...] = bulk[...]
-    joint_terms(q, metric, ghost_ref, meta[FACE], 1.0, range(TILES), out)
+    face = meta[FACE]
+    lane = lanes_of(LEN)
+    mine = [turned_back(sent[LEN * n : LEN * n + LEN, :], meta) for n in range(7)]
+    stencils = [face_stencil(ghost_ref[LEN * c : LEN * c + LEN, :]) for c in range(4)]
+    slopes, curves = [one[0] for one in stencils], [one[1] for one in stencils]
+    added = edge_terms(mine[:4], mine[4:], slopes, curves, 1.0)
+
+    @pl.when(face == 2)
+    def _():
+        for c in range(4):
+            out[c, :, 0:128] = out[c, :, 0:128] + jnp.where(lane < 2 * CROSS, added[c], 0.0)
+
+    @pl.when(face == 3)
+    def _():
+        where = slice(128 * (TILES - 1), 128 * TILES)
+        for c in range(4):
+            value = jnp.where(lane >= 80, pltpu.roll(added[c], 80, 1), pltpu.roll(added[c], 112, 1))
+            out[c, :, where] = out[c, :, where] + jnp.where(lane >= 32, value, 0.0)
+
+    @pl.when(face >= 4)
+    def _():
+        for t in range(TILES):
+            where = slice(128 * t, 128 * t + 128)
+            flat = 128 * t + lane
+            j = flat // CROSS
+            k = flat - j * CROSS
+            depth = jnp.where(face == 4, k, CROSS - 1 - k)
+            index = jnp.where(depth == 0, j, j + CROSS)[:8]
+            for c in range(4):
+                value = jnp.where(depth < 2, gather_lanes(added[c], index), 0.0)
+                out[c, :, where] = out[c, :, where] + value
+
     write_chain(out, even_ref, odd_ref, meta[POSITION])
     even = lax.rem(meta[POSITION], 2) == 0
     spare = slice(CELLS, CELLS + 128)
@@ -582,7 +621,7 @@
     q1, even, odd = local(
         joint_kernel,
         [FIELD] + [f32((8, CELLS + 128))] * 2,
-        (part, q, geometry, one, two, three, mate, meta),
+        (part, joint, one, two, three, mate, meta),
         [GHOST, TILE, TILE],
     )
     from_even, from_odd = along_chain(even, odd)

time: 33.8 us -> 33.9 us (level)
  the two profiles are of different devices: /device:TPU:111 before, /device:TPU:105 now
where the time goes in v2:
time: 33.9 us; the launch traced here: 33.7 us
  starting transfers between devices  16.3 us (48%)
  Pallas kernels  13.1 us (39%)
  waiting for transfers between devices  4.19 us (12%)
    pallas_call x5, Pallas kernels, local(): pl.pallas_call(kernel, out_shape=shapes, in_specs=[VMEM] * (len(operands)...  10.6 us
    ppermute x2, starting transfers between devices, along_chain(): from_odd = lax.ppermute(odd, 'blk', pairs + [(b, a) for a, b in pairs])  10.4 us
    ppermute x3, starting transfers between devices, on_device(): lax.ppermute(value, 'seg', [(i, i ^ s) for i in range(SEGS)])  3.78 us
    ppermute x3, waiting for transfers between devices, on_device(): lax.ppermute(value, 'seg', [(i, i ^ s) for i in range(SEGS)])  2.91 us
    pallas_call x1, Pallas kernels, on_device(): pl.pallas_call(first_kernel, out_shape=[FIELD, f32((9, LEN, CELLS)), JOIN...  2.52 us
    ppermute x1, starting transfers between devices, on_device(): mate = lax.ppermute(picked, 'seg', [(i, i ^ 4) for i in range(SEGS)])  2.1 us
    ppermute x2, waiting for transfers between devices, along_chain(): lax.ppermute(even, 'blk', [(i, i ^ 1) for i in range(CHAIN)])  1.27 us
  transfers between devices with their start and end apart: 8, of which 2 were waited for; matrix products, arithmetic and copies ran while one was open for 0% of the time, Pallas kernels for 19%

profile of v2, /device:TPU:105, one launch (start us, length us, event | category | flops | bytes accessed | tf_op | source)
XLA Modules:
  0.0 33.7 jit_solution(6365131159760038278)
XLA Ops:
  0.0 2.5 %shard_map.46 = (f32[4,16,2304]{2,1,0:T(8,128)S(1)}, f32[9,16,2304]{2,1,0:T(8,128)S(1)}, f32[160,128]{1,0:T(8,128)S(1)}, f32[8,2304]{1,0:T(8,128)S(1)}, f32[8,2304]{1,0:T(8,128)S(1)}, /*index=5*/s32[16]{0:T(128)S(1)}) custom-call(f32[4,16,2304]{2,1,0:T(8,128)} %bitcast.5, f32[9,16,2304]{2,1,0:T(8,128)} %bitcast.4, s32[256]{0:T(256)} %map_hbm.1, ...), custom_call_target="tpu_custom_call" | custom-call | tf_op jit(solution)/shard_map/pallas_call | solution.py:598
  2.5 5.2 %collective-permute-start = (f32[8,2304]{1,0:T(8,128)S(1)}, f32[8,2304]{1,0:T(8,128)S(1)}, u32[]{:S(2)}, u32[]{:S(2)}) collective-permute-start(f32[8,2304]{1,0:T(8,128)S(1)} %get-tuple-element.25), channel_id=1, source_target_pairs={{1,2},{3,4},{5,6},{7,8},{9,10},{11,12},{13,14},{15,16},{17,18},{19... | collective-permute-start | bytes 221192 | tf_op jit(solution)/shard_map/ppermute | solution.py:590
  7.7 2.6 %collective-permute-start.3 = (f32[160,128]{1,0:T(8,128)S(1)}, f32[160,128]{1,0:T(8,128)S(1)}, u32[]{:S(2)}, u32[]{:S(2)}) collective-permute-start(f32[160,128]{1,0:T(8,128)S(1)} %get-tuple-element.26.own.sent), channel_id=1, source_target_pairs={{0,96},{32,64},{64,32},{96,0},{128,224},{160,192},{192,160},{224,1... | collective-permute-start | bytes 245768 | tf_op jit(solution)/shard_map/ppermute | solution.py:611
  10.3 0.5 %collective-permute-start.2 = (f32[160,128]{1,0:T(8,128)S(1)}, f32[160,128]{1,0:T(8,128)S(1)}, u32[]{:S(2)}, u32[]{:S(2)}) collective-permute-start(f32[160,128]{1,0:T(8,128)S(1)} %get-tuple-element.26.own.sent), channel_id=1, source_target_pairs={{0,64},{32,96},{64,0},{96,32},{128,192},{160,224},{192,128},{224,1... | collective-permute-start | bytes 245768 | tf_op jit(solution)/shard_map/ppermute | solution.py:611
  10.8 0.0 collective-permute-done.rest_1_
  10.8 0.7 %collective-permute-start.1 = (f32[160,128]{1,0:T(8,128)S(1)}, f32[160,128]{1,0:T(8,128)S(1)}, u32[]{:S(2)}, u32[]{:S(2)}) collective-permute-start(f32[160,128]{1,0:T(8,128)S(1)} %get-tuple-element.26.own.sent), channel_id=1, source_target_pairs={{0,32},{32,0},{64,96},{96,64},{128,160},{160,128},{192,224},{224,1... | collective-permute-start | bytes 245768 | tf_op jit(solution)/shard_map/ppermute | solution.py:611
  11.5 0.0 collective-permute-start.4
  11.5 1.3 %collective-permute-done.4.rest_0_ = f32[8,2304]{1,0:T(8,128)S(1)} collective-permute-done((f32[8,2304]{1,0:T(8,128)S(1)}, f32[8,2304]{1,0:T(8,128)S(1)}, u32[]{:S(2)}, u32[]{:S(2)}) %collective-permute-start.4) | collective-permute-done | bytes 73760 | tf_op jit(solution)/shard_map/ppermute | solution.py:591
  12.8 0.0 collective-permute-done.3.three
  12.8 2.9 %collective-permute-done.2.two = f32[160,128]{1,0:T(8,128)S(1)} collective-permute-done((f32[160,128]{1,0:T(8,128)S(1)}, f32[160,128]{1,0:T(8,128)S(1)}, u32[]{:S(2)}, u32[]{:S(2)}) %collective-permute-start.2) | collective-permute-done | bytes 81952 | tf_op jit(solution)/shard_map/ppermute | solution.py:611
  15.7 0.0 collective-permute-done.1.one
  15.7 0.6 %shard_map.47 = f32[160,128]{1,0:T(8,128)S(1)} custom-call(f32[160,128]{1,0:T(8,128)S(1)} %get-tuple-element.26.own.sent, f32[160,128]{1,0:T(8,128)S(1)} %collective-permute-done.1.one, f32[160,128]{1,0:T(8,128)S(1)} %collective-permute-done.2.two, f32[160,128]{1,0:T(8,128)S(1)} %collective-permute-done.3.three, s32[16]{0:T(128)S(1)} %get-tuple-element.33.meta.rest_2_.rest_1_), custom_call_target="tpu_custom_call" | custom-call | flops 1000000 | bytes 1000000 | tf_op jit(solution)/shard_map/pallas_call | solution.py:572
  16.3 2.1 %collective-permute-start.5 = (f32[160,128]{1,0:T(8,128)S(1)}, f32[160,128]{1,0:T(8,128)S(1)}, u32[]{:S(2)}, u32[]{:S(2)}) collective-permute-start(f32[160,128]{1,0:T(8,128)S(1)} %shard_map.47), channel_id=1, source_target_pairs={{0,128},{32,160},{64,192},{96,224},{128,0},{160,32},{192,64},{224,... | collective-permute-start | bytes 245768 | tf_op jit(solution)/shard_map/ppermute | solution.py:618
  18.4 3.2 %shard_map.48.bulk = f32[4,16,2304]{2,1,0:T(8,128)S(1)} custom-call(f32[4,16,2304]{2,1,0:T(8,128)S(1)} %get-tuple-element.22.q.rest_0_, f32[9,16,2304]{2,1,0:T(8,128)S(1)} %get-tuple-element.23.metric, f32[8,2304]{1,0:T(8,128)S(1)} %collective-permute-done.4.rest_0_, f32[8,2304]{1,0:T(8,128)S(1)} %collective-permute-done.rest_1_, ...), custom_call_target="tpu_custom_call" | custom-call | flops 12000000 | bytes 12000000 | tf_op jit(solution)/shard_map/pallas_call | solution.py:572
  21.6 0.0 collective-permute-done.5.mate
  21.7 1.1 %shard_map.49 = (f32[4,16,2304]{2,1,0:T(8,128)S(1)}, f32[8,2432]{1,0:T(8,128)S(1)}, f32[8,2432]{1,0:T(8,128)S(1)}) custom-call(f32[4,16,2304]{2,1,0:T(8,128)S(1)} %shard_map.48.bulk, f32[160,128]{1,0:T(8,128)S(1)} %get-tuple-element.26.own.sent, f32[160,128]{1,0:T(8,128)S(1)} %collective-permute-done.1.one, f32[160,128]{1,0:T(8,128)S(1)} %collective-permute-done.2.two, ...), custom_call_target="tpu_custom_call" | custom-call | flops 1000000 | bytes 1000000 | tf_op jit(solution)/shard_map/pallas_call | solution.py:572
  22.7 0.1 collective-permute-start.6
  22.8 5.2 %collective-permute-start.7 = (f32[8,2432]{1,0:T(8,128)S(1)}, f32[8,2432]{1,0:T(8,128)S(1)}, u32[]{:S(2)}, u32[]{:S(2)}) collective-permute-start(f32[8,2432]{1,0:T(8,128)S(1)} %get-tuple-element.38), channel_id=1, source_target_pairs={{1,2},{3,4},{5,6},{7,8},{9,10},{11,12},{13,14},{15,16},{17,18},{19... | collective-permute-start | bytes 233480 | tf_op jit(solution)/shard_map/ppermute | solution.py:590
  28.0 3.2 %shard_map.50.part = f32[4,16,2304]{2,1,0:T(8,128)S(1)} custom-call(f32[4,16,2304]{2,1,0:T(8,128)S(1)} %get-tuple-element.36.q, f32[9,16,2304]{2,1,0:T(8,128)S(1)} %get-tuple-element.23.metric, f32[4,16,2304]{2,1,0:T(8,128)S(1)} %get-tuple-element.22.q.rest_0_, s32[16]{0:T(128)S(1)} %get-tuple-element.33.meta.rest_2_.rest_1_), custom_call_target="tpu_custom_call" | custom-call | flops 12000000 | bytes 12000000 | tf_op jit(solution)/shard_map/pallas_call | solution.py:572
  31.2 0.0 collective-permute-done.6.even_in
  31.2 0.0 collective-permute-done.7.odd_in
  31.2 2.5 %shard_map.51 = f32[4,16,2304]{2,1,0:T(8,128)} custom-call(f32[4,16,2304]{2,1,0:T(8,128)S(1)} %shard_map.50.part, f32[160,128]{1,0:T(8,128)S(1)} %get-tuple-element.26.own.sent, f32[4,16,2304]{2,1,0:T(8,128)S(1)} %get-tuple-element.36.q, f32[9,16,2304]{2,1,0:T(8,128)S(1)} %get-tuple-element.23.metric, f32[160,128]{1,0:T(8,128)S(1)} %collective-permute-done.1.one, ...), custom_call_target="tpu_custom_call" | custom-call | flops 1000000 | bytes 1000000 | tf_op jit(solution)/shard_map/pallas_call | solution.py:572
Async XLA Ops:
  2.5 8.3 %collective-permute-start = (f32[8,2304]{1,0:T(8,128)S(1)}, f32[8,2304]{1,0:T(8,128)S(1)}, u32[]{:S(2)}, u32[]{:S(2)}) collective-permute-start(f32[8,2304]{1,0:T(8,128)S(1)} %get-tuple-element.25), channel_id=1, source_target_pairs={{1,2},{3,4},{5,6},{7,8},{9,10},{11,12},{13,14},{15,16},{17,18},{19... | collective-permute-start | bytes 221192 | tf_op jit(solution)/shard_map/ppermute | solution.py:590
  7.7 5.1 %collective-permute-start.3 = (f32[160,128]{1,0:T(8,128)S(1)}, f32[160,128]{1,0:T(8,128)S(1)}, u32[]{:S(2)}, u32[]{:S(2)}) collective-permute-start(f32[160,128]{1,0:T(8,128)S(1)} %get-tuple-element.26.own.sent), channel_id=1, source_target_pairs={{0,96},{32,64},{64,32},{96,0},{128,224},{160,192},{192,160},{224,1... | collective-permute-start | bytes 245768 | tf_op jit(solution)/shard_map/ppermute | solution.py:611
  10.3 5.4 %collective-permute-start.2 = (f32[160,128]{1,0:T(8,128)S(1)}, f32[160,128]{1,0:T(8,128)S(1)}, u32[]{:S(2)}, u32[]{:S(2)}) collective-permute-start(f32[160,128]{1,0:T(8,128)S(1)} %get-tuple-element.26.own.sent), channel_id=1, source_target_pairs={{0,64},{32,96},{64,0},{96,32},{128,192},{160,224},{192,128},{224,1... | collective-permute-start | bytes 245768 | tf_op jit(solution)/shard_map/ppermute | solution.py:611
  10.8 4.9 %collective-permute-start.1 = (f32[160,128]{1,0:T(8,128)S(1)}, f32[160,128]{1,0:T(8,128)S(1)}, u32[]{:S(2)}, u32[]{:S(2)}) collective-permute-start(f32[160,128]{1,0:T(8,128)S(1)} %get-tuple-element.26.own.sent), channel_id=1, source_target_pairs={{0,32},{32,0},{64,96},{96,64},{128,160},{160,128},{192,224},{224,1... | collective-permute-start | bytes 245768 | tf_op jit(solution)/shard_map/ppermute | solution.py:611
  11.5 1.3 %collective-permute-start.4 = (f32[8,2304]{1,0:T(8,128)S(1)}, f32[8,2304]{1,0:T(8,128)S(1)}, u32[]{:S(2)}, u32[]{:S(2)}) collective-permute-start(f32[8,2304]{1,0:T(8,128)S(1)} %get-tuple-element.27), channel_id=1, source_target_pairs={{0,1},{1,0},{2,3},{3,2},{4,5},{5,4},{6,7},{7,6},{8,9},{9,8},{10,11... | collective-permute-start | bytes 221192 | tf_op jit(solution)/shard_map/ppermute | solution.py:591
  16.3 5.3 %collective-permute-start.5 = (f32[160,128]{1,0:T(8,128)S(1)}, f32[160,128]{1,0:T(8,128)S(1)}, u32[]{:S(2)}, u32[]{:S(2)}) collective-permute-start(f32[160,128]{1,0:T(8,128)S(1)} %shard_map.47), channel_id=1, source_target_pairs={{0,128},{32,160},{64,192},{96,224},{128,0},{160,32},{192,64},{224,... | collective-permute-start | bytes 245768 | tf_op jit(solution)/shard_map/ppermute | solution.py:618
  22.7 8.5 %collective-permute-start.6 = (f32[8,2432]{1,0:T(8,128)S(1)}, f32[8,2432]{1,0:T(8,128)S(1)}, u32[]{:S(2)}, u32[]{:S(2)}) collective-permute-start(f32[8,2432]{1,0:T(8,128)S(1)} %get-tuple-element.37), channel_id=1, source_target_pairs={{0,1},{1,0},{2,3},{3,2},{4,5},{5,4},{6,7},{7,6},{8,9},{9,8},{10,11... | collective-permute-start | bytes 233480 | tf_op jit(solution)/shard_map/ppermute | solution.py:591
  22.8 8.4 %collective-permute-start.7 = (f32[8,2432]{1,0:T(8,128)S(1)}, f32[8,2432]{1,0:T(8,128)S(1)}, u32[]{:S(2)}, u32[]{:S(2)}) collective-permute-start(f32[8,2432]{1,0:T(8,128)S(1)} %get-tuple-element.38), channel_id=1, source_target_pairs={{1,2},{3,4},{5,6},{7,8},{9,10},{11,12},{13,14},{15,16},{17,18},{19... | collective-permute-start | bytes 233480 | tf_op jit(solution)/shard_map/ppermute | solution.py:590

commit v3 on v2

--- a/solution.py
+++ b/solution.py
@@ -407,7 +407,7 @@
             out[c, 8:16, where] = base[c, 8:16, where] + jnp.where(start, 0.0, added[c])
 
 
-def joint_terms(q, metric, ghost_ref, face, scale, tiles, out):
+def joint_terms(q, metric, ghost_ref, spread_ref, face, scale, tiles, out):
     lane = lanes_of(LEN)
 
     def add(t, direction, slopes, curves):
@@ -448,21 +448,16 @@
 
     @pl.when(face >= 4)
     def _():
-        toward = jnp.where(face == 4, -1.0, 1.0)
         for t in tiles:
+            where = slice(128 * t, 128 * t + 128)
             flat = 128 * t + lane
             j = flat // CROSS
             k = flat - j * CROSS
             depth = jnp.where(face == 4, k, CROSS - 1 - k)
-            far = jnp.where(depth == 0, j + CROSS, j)[:8]
-            slopes, curves = [], []
+            index = jnp.where(depth == 0, j, j + CROSS)[:8]
             for c in range(4):
-                ghost = ghost_of(c)
-                first = jnp.where(depth == 0, gather_lanes(ghost, j[:8]), 0.0)
-                second = jnp.where(depth < 2, gather_lanes(ghost, far), 0.0)
-                slopes.append(toward * (8.0 * first - second))
-                curves.append(16.0 * first - second)
-            add(t, 2, slopes, curves)
+                value = gather_lanes(spread_ref[LEN * c : LEN * c + LEN, :], index)
+                out[c, :, where] = out[c, :, where] + jnp.where(depth < 2, value, 0.0)
 
 
 def turned_back(values, meta):
@@ -538,19 +533,30 @@
 
 
 def last_kernel(part, sent, q, metric, one, two, three, mate, even_in, odd_in, meta, out_hbm, *scratch):
-    chain_ref, ghost_ref, main, ends_ref, out, sem = scratch
+    chain_ref, ghost_ref, spread_ref, main, ends_ref, out, sem = scratch
     even = lax.rem(meta[POSITION], 2) == 0
     copy_part(meta[OWN], (mate, one, two, three), PARTS[0], main)
     spare = slice(CELLS, CELLS + 128)
     from_even, from_odd = even_in[:, spare], odd_in[:, spare]
     from_low, from_high = jnp.where(even, from_odd, from_even), jnp.where(even, from_even, from_odd)
     partner_face(sent, main, ends_ref, from_low, from_high, meta, ghost_ref)
+
+    @pl.when(meta[FACE] >= 4)
+    def _():
+        source = face_source(meta[FACE], 0, 0)
+        own = [gather_face(lambda t: q[c, :, 128 * t : 128 * t + 128], source) for c in range(4)]
+        inward = [turned_back(sent[LEN * n : LEN * n + LEN, :], meta) for n in range(4, 7)]
+        stencils = [face_stencil(ghost_ref[LEN * c : LEN * c + LEN, :]) for c in range(4)]
+        added = edge_terms(own, inward, [pair[0] for pair in stencils], [pair[1] for pair in stencils], 0.5)
+        for c in range(4):
+            spread_ref[LEN * c : LEN * c + LEN, :] = added[c]
+
     spread_ghosts(even_in, odd_in, meta, chain_ref)
     copies = []
     for n in range(TILES // GROUP):
         tiles = range(GROUP * n, GROUP * n + GROUP)
         chain_terms(q, metric, chain_ref, 0.5, tiles, part, out)
-        joint_terms(q, metric, ghost_ref, meta[FACE], 0.5, tiles, out)
+        joint_terms(q, metric, ghost_ref, spread_ref, meta[FACE], 0.5, tiles, out)
         where = slice(128 * GROUP * n, 128 * GROUP * (n + 1))
         copies.append(pltpu.make_async_copy(out.at[:, :, where], out_hbm.at[:, :, where], sem.at[n]))
         copies[-1].start()
@@ -630,7 +636,7 @@
         last_kernel,
         [FIELD],
         (part, joint, q1, geometry, one, two, three, mate, from_even, from_odd, meta),
-        [CHAIN_TILES, GHOST, pltpu.VMEM((BELOW, 128), jnp.float32), pltpu.VMEM((7, 8, 128), jnp.float32)]
+        [CHAIN_TILES, GHOST, GHOST, pltpu.VMEM((BELOW, 128), jnp.float32), pltpu.VMEM((7, 8, 128), jnp.float32)]
         + [pltpu.VMEM((4, LEN, CELLS), jnp.float32), pltpu.SemaphoreType.DMA((TILES // GROUP,))],
         out_specs=[HBM],
     )

time: 33.9 us -> 33.9 us (level)
  no operation moved by 1% of the time
where the time goes in v3:
time: 33.9 us
  starting transfers between devices  16.6 us (49%)
  Pallas kernels  13 us (38%)
  waiting for transfers between devices  4.19 us (12%)
    ppermute x2, starting transfers between devices, along_chain(): from_odd = lax.ppermute(odd, 'blk', pairs + [(b, a) for a, b in pairs])  10.6 us
    pallas_call x5, Pallas kernels, local(): pl.pallas_call(kernel, out_shape=shapes, in_specs=[VMEM] * (len(operands)...  10.5 us
    ppermute x3, starting transfers between devices, on_device(): lax.ppermute(value, 'seg', [(i, i ^ s) for i in range(SEGS)])  3.78 us
    ppermute x3, waiting for transfers between devices, on_device(): lax.ppermute(value, 'seg', [(i, i ^ s) for i in range(SEGS)])  2.91 us
    pallas_call x1, Pallas kernels, on_device(): pl.pallas_call(first_kernel, out_shape=[FIELD, f32((9, LEN, CELLS)), JOIN...  2.52 us
    ppermute x1, starting transfers between devices, on_device(): mate = lax.ppermute(picked, 'seg', [(i, i ^ 4) for i in range(SEGS)])  2.1 us
    ppermute x2, waiting for transfers between devices, along_chain(): lax.ppermute(even, 'blk', [(i, i ^ 1) for i in range(CHAIN)])  1.27 us
  transfers between devices with their start and end apart: 8, of which 2 were waited for; matrix products, arithmetic and copies ran while one was open for 0% of the time, Pallas kernels for 19%

profile of v3, /device:TPU:105, one launch (start us, length us, event | category | flops | bytes accessed | tf_op | source)
XLA Modules:
  0.0 33.9 jit_solution(6873370274632384256)
XLA Ops:
  0.0 2.5 %shard_map.46 = (f32[4,16,2304]{2,1,0:T(8,128)S(1)}, f32[9,16,2304]{2,1,0:T(8,128)S(1)}, f32[160,128]{1,0:T(8,128)S(1)}, f32[8,2304]{1,0:T(8,128)S(1)}, f32[8,2304]{1,0:T(8,128)S(1)}, /*index=5*/s32[16]{0:T(128)S(1)}) custom-call(f32[4,16,2304]{2,1,0:T(8,128)} %bitcast.5, f32[9,16,2304]{2,1,0:T(8,128)} %bitcast.4, s32[256]{0:T(256)} %map_hbm.1, ...), custom_call_target="tpu_custom_call" | custom-call | tf_op jit(solution)/shard_map/pallas_call | solution.py:604
  2.5 5.2 %collective-permute-start = (f32[8,2304]{1,0:T(8,128)S(1)}, f32[8,2304]{1,0:T(8,128)S(1)}, u32[]{:S(2)}, u32[]{:S(2)}) collective-permute-start(f32[8,2304]{1,0:T(8,128)S(1)} %get-tuple-element.25), channel_id=1, source_target_pairs={{1,2},{3,4},{5,6},{7,8},{9,10},{11,12},{13,14},{15,16},{17,18},{19... | collective-permute-start | bytes 221192 | tf_op jit(solution)/shard_map/ppermute | solution.py:596
  7.7 2.6 %collective-permute-start.3 = (f32[160,128]{1,0:T(8,128)S(1)}, f32[160,128]{1,0:T(8,128)S(1)}, u32[]{:S(2)}, u32[]{:S(2)}) collective-permute-start(f32[160,128]{1,0:T(8,128)S(1)} %get-tuple-element.26.own.sent), channel_id=1, source_target_pairs={{0,96},{32,64},{64,32},{96,0},{128,224},{160,192},{192,160},{224,1... | collective-permute-start | bytes 245768 | tf_op jit(solution)/shard_map/ppermute | solution.py:617
  10.3 0.5 %collective-permute-start.2 = (f32[160,128]{1,0:T(8,128)S(1)}, f32[160,128]{1,0:T(8,128)S(1)}, u32[]{:S(2)}, u32[]{:S(2)}) collective-permute-start(f32[160,128]{1,0:T(8,128)S(1)} %get-tuple-element.26.own.sent), channel_id=1, source_target_pairs={{0,64},{32,96},{64,0},{96,32},{128,192},{160,224},{192,128},{224,1... | collective-permute-start | bytes 245768 | tf_op jit(solution)/shard_map/ppermute | solution.py:617
  10.8 0.0 collective-permute-done.rest_1_
  10.8 0.7 %collective-permute-start.1 = (f32[160,128]{1,0:T(8,128)S(1)}, f32[160,128]{1,0:T(8,128)S(1)}, u32[]{:S(2)}, u32[]{:S(2)}) collective-permute-start(f32[160,128]{1,0:T(8,128)S(1)} %get-tuple-element.26.own.sent), channel_id=1, source_target_pairs={{0,32},{32,0},{64,96},{96,64},{128,160},{160,128},{192,224},{224,1... | collective-permute-start | bytes 245768 | tf_op jit(solution)/shard_map/ppermute | solution.py:617
  11.5 0.0 collective-permute-start.4
  11.5 1.3 %collective-permute-done.4.rest_0_ = f32[8,2304]{1,0:T(8,128)S(1)} collective-permute-done((f32[8,2304]{1,0:T(8,128)S(1)}, f32[8,2304]{1,0:T(8,128)S(1)}, u32[]{:S(2)}, u32[]{:S(2)}) %collective-permute-start.4) | collective-permute-done | bytes 73760 | tf_op jit(solution)/shard_map/ppermute | solution.py:597
  12.8 0.0 collective-permute-done.3.three
  12.8 2.9 %collective-permute-done.2.two = f32[160,128]{1,0:T(8,128)S(1)} collective-permute-done((f32[160,128]{1,0:T(8,128)S(1)}, f32[160,128]{1,0:T(8,128)S(1)}, u32[]{:S(2)}, u32[]{:S(2)}) %collective-permute-start.2) | collective-permute-done | bytes 81952 | tf_op jit(solution)/shard_map/ppermute | solution.py:617
  15.7 0.0 collective-permute-done.1.one
  15.7 0.6 %shard_map.47 = f32[160,128]{1,0:T(8,128)S(1)} custom-call(f32[160,128]{1,0:T(8,128)S(1)} %get-tuple-element.26.own.sent, f32[160,128]{1,0:T(8,128)S(1)} %collective-permute-done.1.one, f32[160,128]{1,0:T(8,128)S(1)} %collective-permute-done.2.two, f32[160,128]{1,0:T(8,128)S(1)} %collective-permute-done.3.three, s32[16]{0:T(128)S(1)} %get-tuple-element.33.meta.rest_2_.rest_1_), custom_call_target="tpu_custom_call" | custom-call | flops 1000000 | bytes 1000000 | tf_op jit(solution)/shard_map/pallas_call | solution.py:578
  16.3 2.1 %collective-permute-start.5 = (f32[160,128]{1,0:T(8,128)S(1)}, f32[160,128]{1,0:T(8,128)S(1)}, u32[]{:S(2)}, u32[]{:S(2)}) collective-permute-start(f32[160,128]{1,0:T(8,128)S(1)} %shard_map.47), channel_id=1, source_target_pairs={{0,128},{32,160},{64,192},{96,224},{128,0},{160,32},{192,64},{224,... | collective-permute-start | bytes 245768 | tf_op jit(solution)/shard_map/ppermute | solution.py:624
  18.4 3.2 %shard_map.48.bulk = f32[4,16,2304]{2,1,0:T(8,128)S(1)} custom-call(f32[4,16,2304]{2,1,0:T(8,128)S(1)} %get-tuple-element.22.q.rest_0_, f32[9,16,2304]{2,1,0:T(8,128)S(1)} %get-tuple-element.23.metric, f32[8,2304]{1,0:T(8,128)S(1)} %collective-permute-done.4.rest_0_, f32[8,2304]{1,0:T(8,128)S(1)} %collective-permute-done.rest_1_, ...), custom_call_target="tpu_custom_call" | custom-call | flops 12000000 | bytes 12000000 | tf_op jit(solution)/shard_map/pallas_call | solution.py:578
  21.6 0.0 collective-permute-done.5.mate
  21.7 1.1 %shard_map.49 = (f32[4,16,2304]{2,1,0:T(8,128)S(1)}, f32[8,2432]{1,0:T(8,128)S(1)}, f32[8,2432]{1,0:T(8,128)S(1)}) custom-call(f32[4,16,2304]{2,1,0:T(8,128)S(1)} %shard_map.48.bulk, f32[160,128]{1,0:T(8,128)S(1)} %get-tuple-element.26.own.sent, f32[160,128]{1,0:T(8,128)S(1)} %collective-permute-done.1.one, f32[160,128]{1,0:T(8,128)S(1)} %collective-permute-done.2.two, ...), custom_call_target="tpu_custom_call" | custom-call | flops 1000000 | bytes 1000000 | tf_op jit(solution)/shard_map/pallas_call | solution.py:578
  22.7 0.1 collective-permute-start.6
  22.8 5.4 %collective-permute-start.7 = (f32[8,2432]{1,0:T(8,128)S(1)}, f32[8,2432]{1,0:T(8,128)S(1)}, u32[]{:S(2)}, u32[]{:S(2)}) collective-permute-start(f32[8,2432]{1,0:T(8,128)S(1)} %get-tuple-element.38), channel_id=1, source_target_pairs={{1,2},{3,4},{5,6},{7,8},{9,10},{11,12},{13,14},{15,16},{17,18},{19... | collective-permute-start | bytes 233480 | tf_op jit(solution)/shard_map/ppermute | solution.py:596
  28.3 3.2 %shard_map.50.part = f32[4,16,2304]{2,1,0:T(8,128)S(1)} custom-call(f32[4,16,2304]{2,1,0:T(8,128)S(1)} %get-tuple-element.36.q, f32[9,16,2304]{2,1,0:T(8,128)S(1)} %get-tuple-element.23.metric, f32[4,16,2304]{2,1,0:T(8,128)S(1)} %get-tuple-element.22.q.rest_0_, s32[16]{0:T(128)S(1)} %get-tuple-element.33.meta.rest_2_.rest_1_), custom_call_target="tpu_custom_call" | custom-call | flops 12000000 | bytes 12000000 | tf_op jit(solution)/shard_map/pallas_call | solution.py:578
  31.5 0.0 collective-permute-done.6.even_in
  31.5 0.0 collective-permute-done.7.odd_in
  31.5 2.4 %shard_map.51 = f32[4,16,2304]{2,1,0:T(8,128)} custom-call(f32[4,16,2304]{2,1,0:T(8,128)S(1)} %shard_map.50.part, f32[160,128]{1,0:T(8,128)S(1)} %get-tuple-element.26.own.sent, f32[4,16,2304]{2,1,0:T(8,128)S(1)} %get-tuple-element.36.q, f32[9,16,2304]{2,1,0:T(8,128)S(1)} %get-tuple-element.23.metric, f32[160,128]{1,0:T(8,128)S(1)} %collective-permute-done.1.one, ...), custom_call_target="tpu_custom_call" | custom-call | flops 1000000 | bytes 1000000 | tf_op jit(solution)/shard_map/pallas_call | solution.py:578
Async XLA Ops:
  2.5 8.3 %collective-permute-start = (f32[8,2304]{1,0:T(8,128)S(1)}, f32[8,2304]{1,0:T(8,128)S(1)}, u32[]{:S(2)}, u32[]{:S(2)}) collective-permute-start(f32[8,2304]{1,0:T(8,128)S(1)} %get-tuple-element.25), channel_id=1, source_target_pairs={{1,2},{3,4},{5,6},{7,8},{9,10},{11,12},{13,14},{15,16},{17,18},{19... | collective-permute-start | bytes 221192 | tf_op jit(solution)/shard_map/ppermute | solution.py:596
  7.7 5.1 %collective-permute-start.3 = (f32[160,128]{1,0:T(8,128)S(1)}, f32[160,128]{1,0:T(8,128)S(1)}, u32[]{:S(2)}, u32[]{:S(2)}) collective-permute-start(f32[160,128]{1,0:T(8,128)S(1)} %get-tuple-element.26.own.sent), channel_id=1, source_target_pairs={{0,96},{32,64},{64,32},{96,0},{128,224},{160,192},{192,160},{224,1... | collective-permute-start | bytes 245768 | tf_op jit(solution)/shard_map/ppermute | solution.py:617
  10.3 5.4 %collective-permute-start.2 = (f32[160,128]{1,0:T(8,128)S(1)}, f32[160,128]{1,0:T(8,128)S(1)}, u32[]{:S(2)}, u32[]{:S(2)}) collective-permute-start(f32[160,128]{1,0:T(8,128)S(1)} %get-tuple-element.26.own.sent), channel_id=1, source_target_pairs={{0,64},{32,96},{64,0},{96,32},{128,192},{160,224},{192,128},{224,1... | collective-permute-start | bytes 245768 | tf_op jit(solution)/shard_map/ppermute | solution.py:617
  10.8 4.9 %collective-permute-start.1 = (f32[160,128]{1,0:T(8,128)S(1)}, f32[160,128]{1,0:T(8,128)S(1)}, u32[]{:S(2)}, u32[]{:S(2)}) collective-permute-start(f32[160,128]{1,0:T(8,128)S(1)} %get-tuple-element.26.own.sent), channel_id=1, source_target_pairs={{0,32},{32,0},{64,96},{96,64},{128,160},{160,128},{192,224},{224,1... | collective-permute-start | bytes 245768 | tf_op jit(solution)/shard_map/ppermute | solution.py:617
  11.5 1.3 %collective-permute-start.4 = (f32[8,2304]{1,0:T(8,128)S(1)}, f32[8,2304]{1,0:T(8,128)S(1)}, u32[]{:S(2)}, u32[]{:S(2)}) collective-permute-start(f32[8,2304]{1,0:T(8,128)S(1)} %get-tuple-element.27), channel_id=1, source_target_pairs={{0,1},{1,0},{2,3},{3,2},{4,5},{5,4},{6,7},{7,6},{8,9},{9,8},{10,11... | collective-permute-start | bytes 221192 | tf_op jit(solution)/shard_map/ppermute | solution.py:597
  16.3 5.3 %collective-permute-start.5 = (f32[160,128]{1,0:T(8,128)S(1)}, f32[160,128]{1,0:T(8,128)S(1)}, u32[]{:S(2)}, u32[]{:S(2)}) collective-permute-start(f32[160,128]{1,0:T(8,128)S(1)} %shard_map.47), channel_id=1, source_target_pairs={{0,128},{32,160},{64,192},{96,224},{128,0},{160,32},{192,64},{224,... | collective-permute-start | bytes 245768 | tf_op jit(solution)/shard_map/ppermute | solution.py:624
  22.7 8.7 %collective-permute-start.6 = (f32[8,2432]{1,0:T(8,128)S(1)}, f32[8,2432]{1,0:T(8,128)S(1)}, u32[]{:S(2)}, u32[]{:S(2)}) collective-permute-start(f32[8,2432]{1,0:T(8,128)S(1)} %get-tuple-element.37), channel_id=1, source_target_pairs={{0,1},{1,0},{2,3},{3,2},{4,5},{5,4},{6,7},{7,6},{8,9},{9,8},{10,11... | collective-permute-start | bytes 233480 | tf_op jit(solution)/shard_map/ppermute | solution.py:597
  22.8 8.7 %collective-permute-start.7 = (f32[8,2432]{1,0:T(8,128)S(1)}, f32[8,2432]{1,0:T(8,128)S(1)}, u32[]{:S(2)}, u32[]{:S(2)}) collective-permute-start(f32[8,2432]{1,0:T(8,128)S(1)} %get-tuple-element.38), channel_id=1, source_target_pairs={{1,2},{3,4},{5,6},{7,8},{9,10},{11,12},{13,14},{15,16},{17,18},{19... | collective-permute-start | bytes 233480 | tf_op jit(solution)/shard_map/ppermute | solution.py:596
